TPU v7x, 32 devices: a whole 2x2x4 slice. The times are simulated.
32 devices in a mesh: dp: 8 (over z, y), mp: 4 (over x, core).
Axes of the slice: x: 2, y: 2, z: 4, core: 2. Of those that a mesh axis runs over, the one named last changes fastest.
Arguments:
- inputs: bfloat16 [2, 8192, 1024], P(None, ('dp', 'mp')), may hold values from -6 to 6
- segments: int32 [2, 8192], P(None, 'dp'), may hold values from 0 to 3, as said below
- query_weight: bfloat16 [1024, 1024], P('dp', 'mp'), may hold values from -0.1875 to 0.1875
- key_weight: bfloat16 [1024, 1024], P('dp', 'mp'), may hold values from -0.1875 to 0.1875
- value_weight: bfloat16 [1024, 1024], P('dp', 'mp'), may hold values from -0.1875 to 0.1875
- out_weight: bfloat16 [1024, 1024], P('mp', 'dp'), may hold values from -3 to 3
- up_weight: bfloat16 [1024, 4096], P('dp', 'mp'), may hold values from -0.1875 to 0.1875
- down_weight: bfloat16 [4096, 1024], P('mp', 'dp'), may hold values from -0.09375 to 0.09375
- query_bias: float32 [1024], replicated, may hold values from -3 to 3
- value_bias: float32 [1024], replicated, may hold values from -0.3 to 0.3
- out_bias: float32 [1024], replicated, may hold values from -3 to 3
- up_bias: float32 [4096], replicated, may hold values from -3 to 3
- down_bias: float32 [1024], replicated, may hold values from -3 to 3
- first_gain: float32 [1024], replicated, may hold values from 0.25 to 1.75
- first_shift: float32 [1024], replicated, may hold values from -3 to 3
- second_gain: float32 [1024], replicated, may hold values from 0.25 to 1.75
- second_shift: float32 [1024], replicated, may hold values from -3 to 3
- cotangent: bfloat16 [2, 8192, 1024], P(None, ('dp', 'mp')), may hold values from -6 to 6
Outputs:
- outputs: bfloat16 [2, 8192, 1024], P(None, ('dp', 'mp'))
- input_grad: float32 [2, 8192, 1024], P(None, ('dp', 'mp'))
- grad_query: float32 [1024, 1024], P('dp', 'mp')
- grad_key: float32 [1024, 1024], P('dp', 'mp')
- grad_value: float32 [1024, 1024], P('dp', 'mp')
- grad_out: float32 [1024, 1024], P('mp', 'dp')
- grad_up: float32 [1024, 4096], P('dp', 'mp')
- grad_down: float32 [4096, 1024], P('mp', 'dp')
- grad_query_bias: float32 [1024], replicated
- grad_value_bias: float32 [1024], replicated
- grad_out_bias: float32 [1024], replicated
- grad_up_bias: float32 [4096], replicated
- grad_down_bias: float32 [1024], replicated
- grad_first_gain: float32 [1024], replicated
- grad_first_shift: float32 [1024], replicated
- grad_second_gain: float32 [1024], replicated
- grad_second_shift: float32 [1024], replicated
Inputs may be any that keep to these rules, and one draw needn't show every extreme that they name: `segments`: within each aligned block of 1024 positions (one pack) the numbers never fall and all four of 0 to 3 occur; tokens attend only to tokens of their own pack with the same number.
All inputs are finite; a program needn't handle non-finite values.
Results may differ from a plain program's by a relative error of at most 0.018.
Values may be sent and summed in bfloat16 or wider, within the bound.
A program may use at most 192 MiB of HBM per device.

v0:
```python
import jax
import jax.numpy as jnp
from jax import lax
from jax.sharding import PartitionSpec as P

HDIM = 64


epsilon = 1e-06


def matmul(left_mat, right_mat):
    return jnp.dot(left_mat, right_mat, preferred_element_type=jnp.float32)


def inner_rows(left_mat, right_mat):
    return lax.dot_general(
        left_mat, right_mat, (((0,), (0,)), ((), ())), preferred_element_type=jnp.float32
    )


def outer_cols(left_mat, right_mat):
    return lax.dot_general(
        left_mat, right_mat, (((1,), (1,)), ((), ())), preferred_element_type=jnp.float32
    )


def norm_forward(residual, scale_vec, shift_vec):
    mean_val = jnp.mean(residual, axis=-1, keepdims=True)
    centred = residual - mean_val
    inverse = lax.rsqrt(jnp.mean(centred * centred, axis=-1, keepdims=True) + epsilon)
    normed = centred * inverse
    return (normed * scale_vec + shift_vec, normed, inverse)


def norm_backward(incoming, normed, inverse, scale_vec):
    scaled = incoming * scale_vec
    centre_term = jnp.mean(scaled, axis=-1, keepdims=True)
    slope_term = jnp.mean(scaled * normed, axis=-1, keepdims=True)
    return (
        inverse * (scaled - centre_term - normed * slope_term),
        jnp.sum(incoming * normed, axis=0),
        jnp.sum(incoming, axis=0),
    )


def gelu_exact(values_in):
    return jax.nn.gelu(values_in, approximate=False)


def head_major(matrix, head_count):
    return matrix.reshape(matrix.shape[0], head_count, HDIM).transpose(1, 0, 2)


def head_blocks(matrix, head_count, block_rows):
    row_count = matrix.shape[0]
    return (
        head_major(matrix, head_count)
        .reshape(head_count, row_count // block_rows, block_rows, HDIM)
        .transpose(1, 0, 2, 3)
    )


def score_block(query_block, key_heads, query_segs, key_segs):
    raw_scores = jnp.einsum(
        "hqd,hkd->hqk", query_block, key_heads, preferred_element_type=jnp.float32
    )
    same_doc = (query_segs[:, None] == key_segs[None, :])[None]
    return jnp.where(same_doc, raw_scores * HDIM ** (-0.5), -1000000000.0)


def attention_forward(queries, key_rows, value_rows, seg_row, head_count):
    row_count = queries.shape[0]
    block_rows = min(512, row_count)
    key_heads = head_major(key_rows, head_count)
    value_heads = head_major(value_rows, head_count)

    def one_block(pieces):
        query_block, query_segs = pieces
        scores = score_block(query_block, key_heads, query_segs, seg_row)
        top_val = jnp.max(scores, axis=-1, keepdims=True)
        exponent = jnp.exp(scores - top_val)
        totals = jnp.sum(exponent, axis=-1, keepdims=True)
        probabilities = (exponent / totals).astype(jnp.bfloat16)
        context = jnp.einsum(
            "hqk,hkd->hqd", probabilities, value_heads, preferred_element_type=jnp.float32
        )
        return (context, (top_val + jnp.log(totals))[..., 0])

    context, log_totals = lax.map(
        one_block, (head_blocks(queries, head_count, block_rows), seg_row.reshape(-1, block_rows))
    )
    return (context.transpose(0, 2, 1, 3).reshape(row_count, head_count * HDIM), log_totals)


def attention_backward(
    queries, key_rows, value_rows, seg_row, log_totals, grad_context, head_count
):
    row_count = queries.shape[0]
    block_rows = min(512, row_count)
    key_heads = head_major(key_rows, head_count)
    value_heads = head_major(value_rows, head_count)
    scale_val = HDIM ** (-0.5)

    def one_block(sum_pair, pieces):
        query_block, grad_block, query_segs, block_lse = pieces
        scores = score_block(query_block, key_heads, query_segs, seg_row)
        probabilities = jnp.exp(scores - block_lse[..., None])
        grad_probs = jnp.einsum(
            "hqd,hkd->hqk", grad_block, value_heads, preferred_element_type=jnp.float32
        )
        grad_scores = (
            probabilities
            * (grad_probs - jnp.sum(grad_probs * probabilities, axis=-1, keepdims=True))
        ).astype(jnp.bfloat16)
        grad_query = (
            jnp.einsum("hqk,hkd->hqd", grad_scores, key_heads, preferred_element_type=jnp.float32)
            * scale_val
        )
        key_sum = (
            sum_pair[0]
            + jnp.einsum(
                "hqk,hqd->hkd", grad_scores, query_block, preferred_element_type=jnp.float32
            )
            * scale_val
        )
        value_sum = sum_pair[1] + jnp.einsum(
            "hqk,hqd->hkd",
            probabilities.astype(jnp.bfloat16),
            grad_block,
            preferred_element_type=jnp.float32,
        )
        return ((key_sum, value_sum), grad_query)

    zero_acc = jnp.zeros((head_count, row_count, HDIM), jnp.float32)
    pieces = (
        head_blocks(queries, head_count, block_rows),
        head_blocks(grad_context, head_count, block_rows),
        seg_row.reshape(-1, block_rows),
        log_totals,
    )
    (key_sum, value_sum), grad_query = lax.scan(one_block, (zero_acc, zero_acc), pieces)
    grad_query = grad_query.transpose(0, 2, 1, 3).reshape(row_count, head_count * HDIM)
    key_sum = key_sum.transpose(1, 0, 2).reshape(row_count, head_count * HDIM)
    value_sum = value_sum.transpose(1, 0, 2).reshape(row_count, head_count * HDIM)
    return (
        grad_query.astype(jnp.bfloat16),
        key_sum.astype(jnp.bfloat16),
        value_sum.astype(jnp.bfloat16),
    )


def on_device(
    inputs,
    segments,
    query_weight,
    key_weight,
    value_weight,
    out_weight,
    up_weight,
    down_weight,
    query_bias,
    value_bias,
    out_bias,
    up_bias,
    down_bias,
    first_gain,
    first_shift,
    second_gain,
    second_shift,
    cotangent,
):
    micro_count = inputs.shape[0]
    head_cols = query_weight.shape[1]
    unit_cols = up_weight.shape[1]
    head_count = head_cols // HDIM
    mp_rank = lax.axis_index("mp")
    query_bias_own = lax.dynamic_slice_in_dim(query_bias, mp_rank * head_cols, head_cols)
    value_bias_own = lax.dynamic_slice_in_dim(value_bias, mp_rank * head_cols, head_cols)
    up_bias_own = lax.dynamic_slice_in_dim(up_bias, mp_rank * unit_cols, unit_cols)

    def fetch():
        shards = (
            lax.all_gather(query_weight, "dp", axis=0, tiled=True),
            lax.all_gather(key_weight, "dp", axis=0, tiled=True),
            lax.all_gather(value_weight, "dp", axis=0, tiled=True),
            lax.all_gather(up_weight, "dp", axis=0, tiled=True),
            lax.all_gather(out_weight, "dp", axis=1, tiled=True),
            lax.all_gather(down_weight, "dp", axis=1, tiled=True),
        )
        return (shards, None)

    results = []
    saved_list = []
    for micro_index in range(micro_count):
        weights = fetch()
        forward_shards, forward_whole_mats = weights
        (
            forward_query_all,
            forward_key_all,
            forward_value_all,
            forward_up_all,
            forward_out_all,
            forward_down_all,
        ) = forward_shards
        own_tokens = inputs[micro_index]
        forward_seg_row = segments[micro_index]
        forward_token_rows = lax.all_gather(own_tokens, "mp", axis=0, tiled=True)
        forward_queries = (matmul(forward_token_rows, forward_query_all) + query_bias_own).astype(
            jnp.bfloat16
        )
        forward_key_rows = matmul(forward_token_rows, forward_key_all).astype(jnp.bfloat16)
        forward_value_rows = (
            matmul(forward_token_rows, forward_value_all) + value_bias_own
        ).astype(jnp.bfloat16)
        forward_context, forward_log_totals = attention_forward(
            forward_queries, forward_key_rows, forward_value_rows, forward_seg_row, head_count
        )
        forward_context = forward_context.astype(jnp.bfloat16)
        attention_out = lax.psum_scatter(
            matmul(forward_context, forward_out_all), "mp", scatter_dimension=0, tiled=True
        )
        first_out, forward_first_normed, forward_first_inverse = norm_forward(
            own_tokens.astype(jnp.float32) + attention_out + out_bias, first_gain, first_shift
        )
        forward_first_rows = lax.all_gather(
            first_out.astype(jnp.bfloat16), "mp", axis=0, tiled=True
        )
        forward_hidden = matmul(forward_first_rows, forward_up_all) + up_bias_own
        forward_active = gelu_exact(forward_hidden).astype(jnp.bfloat16)
        feed_out = lax.psum_scatter(
            matmul(forward_active, forward_down_all), "mp", scatter_dimension=0, tiled=True
        )
        final_out, forward_second_normed, forward_second_inverse = norm_forward(
            first_out + feed_out + down_bias, second_gain, second_shift
        )
        forward_saved_state = (
            forward_token_rows,
            forward_seg_row,
            forward_queries,
            forward_key_rows,
            forward_value_rows,
            forward_log_totals,
            forward_context,
            forward_first_normed,
            forward_first_inverse,
            forward_first_rows,
            forward_hidden,
            forward_active,
            forward_second_normed,
            forward_second_inverse,
        )
        final_out, saved_state = (final_out.astype(jnp.bfloat16), forward_saved_state)
        results.append(final_out)
        saved_list.append(saved_state)
    weight_sums = None
    vector_sums = None
    input_grads = []
    for micro_index in range(micro_count):
        weights = fetch()
        backward_saved_state = saved_list[micro_index]
        backward_shards, whole_mats = weights
        query_all, key_all, value_all, up_all, out_all, down_all = backward_shards
        (
            token_rows,
            seg_row,
            queries,
            key_rows,
            value_rows,
            log_totals,
            context,
            first_normed,
            first_inverse,
            first_rows,
            hidden,
            active,
            second_normed,
            second_inverse,
        ) = backward_saved_state
        incoming = cotangent[micro_index].astype(jnp.float32)
        grad_second, grad_second_gain, grad_second_shift = norm_backward(
            incoming, second_normed, second_inverse, second_gain
        )
        feed_rows = lax.all_gather(grad_second.astype(jnp.bfloat16), "mp", axis=0, tiled=True)
        backward_grad_down = inner_rows(active, feed_rows)
        grad_active = outer_cols(feed_rows, down_all)
        grad_hidden = jax.vjp(gelu_exact, hidden)[1](grad_active)[0].astype(jnp.bfloat16)
        backward_grad_up = inner_rows(first_rows, grad_hidden)
        grad_first = grad_second + lax.psum_scatter(
            outer_cols(grad_hidden, up_all), "mp", scatter_dimension=0, tiled=True
        )
        grad_resid, grad_first_gain, grad_first_shift = norm_backward(
            grad_first, first_normed, first_inverse, first_gain
        )
        attention_rows = lax.all_gather(grad_resid.astype(jnp.bfloat16), "mp", axis=0, tiled=True)
        backward_grad_out = inner_rows(context, attention_rows)
        grad_context = outer_cols(attention_rows, out_all).astype(jnp.bfloat16)
        grad_queries, grad_keys, grad_values = attention_backward(
            queries, key_rows, value_rows, seg_row, log_totals, grad_context, head_count
        )
        backward_grad_query = inner_rows(token_rows, grad_queries)
        backward_grad_key = inner_rows(token_rows, grad_keys)
        backward_grad_value = inner_rows(token_rows, grad_values)
        token_grad = lax.psum_scatter(
            (
                outer_cols(grad_queries, query_all)
                + outer_cols(grad_keys, key_all)
                + outer_cols(grad_values, value_all)
            ).astype(jnp.bfloat16),
            "mp",
            scatter_dimension=0,
            tiled=True,
        ).astype(jnp.float32)
        weight_terms = (
            backward_grad_query,
            backward_grad_key,
            backward_grad_value,
            backward_grad_up,
            backward_grad_out,
            backward_grad_down,
        )
        vector_terms = (
            jnp.sum(grad_queries.astype(jnp.float32), axis=0),
            jnp.sum(grad_values.astype(jnp.float32), axis=0),
            jnp.sum(grad_resid, axis=0),
            jnp.sum(grad_hidden.astype(jnp.float32), axis=0),
            jnp.sum(grad_second, axis=0),
            grad_first_gain,
            grad_first_shift,
            grad_second_gain,
            grad_second_shift,
        )
        weight_terms, vector_terms, input_part = (
            weight_terms,
            vector_terms,
            grad_resid + token_grad,
        )
        weight_sums = (
            weight_terms
            if weight_sums is None
            else jax.tree.map(jnp.add, weight_sums, weight_terms)
        )
        vector_sums = (
            vector_terms
            if vector_sums is None
            else jax.tree.map(jnp.add, vector_sums, vector_terms)
        )
        input_grads.append(input_part)
    grad_query, grad_key, grad_value, grad_up, grad_out, grad_down = (
        lax.psum_scatter(
            weight_sums[0].astype(jnp.bfloat16), "dp", scatter_dimension=0, tiled=True
        ).astype(jnp.float32),
        lax.psum_scatter(
            weight_sums[1].astype(jnp.bfloat16), "dp", scatter_dimension=0, tiled=True
        ).astype(jnp.float32),
        lax.psum_scatter(
            weight_sums[2].astype(jnp.bfloat16), "dp", scatter_dimension=0, tiled=True
        ).astype(jnp.float32),
        lax.psum_scatter(
            weight_sums[3].astype(jnp.bfloat16), "dp", scatter_dimension=0, tiled=True
        ).astype(jnp.float32),
        lax.psum_scatter(
            weight_sums[4].astype(jnp.bfloat16), "dp", scatter_dimension=1, tiled=True
        ).astype(jnp.float32),
        lax.psum_scatter(
            weight_sums[5].astype(jnp.bfloat16), "dp", scatter_dimension=1, tiled=True
        ).astype(jnp.float32),
    )

    def widen(vector_part, full_size, offset):
        return lax.dynamic_update_slice_in_dim(
            jnp.zeros((full_size,), jnp.float32), vector_part, offset, 0
        )

    query_bias_full = widen(vector_sums[0], query_bias.shape[0], mp_rank * head_cols)
    value_bias_full = widen(vector_sums[1], value_bias.shape[0], mp_rank * head_cols)
    up_bias_full = widen(vector_sums[3], up_bias.shape[0], mp_rank * unit_cols)
    summed = lax.psum(
        (
            query_bias_full,
            value_bias_full,
            vector_sums[2],
            up_bias_full,
            vector_sums[4],
            vector_sums[5],
            vector_sums[6],
            vector_sums[7],
            vector_sums[8],
        ),
        ("dp", "mp"),
    )
    return (
        jnp.stack(results),
        jnp.stack(input_grads),
        grad_query,
        grad_key,
        grad_value,
        grad_out,
        grad_up,
        grad_down,
        summed[0],
        summed[1],
        summed[2],
        summed[3],
        summed[4],
        summed[5],
        summed[6],
        summed[7],
        summed[8],
    )


def solution(mesh):
    in_specs = (
        P(None, ("dp", "mp"), None),
        P(None, "dp"),
        P("dp", "mp"),
        P("dp", "mp"),
        P("dp", "mp"),
        P("mp", "dp"),
        P("dp", "mp"),
        P("mp", "dp"),
        P(),
        P(),
        P(),
        P(),
        P(),
        P(),
        P(),
        P(),
        P(),
        P(None, ("dp", "mp"), None),
    )
    out_specs = (
        P(None, ("dp", "mp"), None),
        P(None, ("dp", "mp"), None),
        P("dp", "mp"),
        P("dp", "mp"),
        P("dp", "mp"),
        P("mp", "dp"),
        P("dp", "mp"),
        P("mp", "dp"),
        P(),
        P(),
        P(),
        P(),
        P(),
        P(),
        P(),
        P(),
        P(),
    )
    return jax.shard_map(
        on_device, mesh=mesh, in_specs=in_specs, out_specs=out_specs, check_vma=False
    )
```

profile of v0, /device:TPU:0, one launch (start us, length us, event | category | flops | bytes accessed | tf_op | source)
XLA Modules:
  0.0 1159.6 jit_solution(6442051679393694094)
XLA Ops:
  13.5 33.3 %all_gather.29 = bf16[1024,256]{1,0:T(8,128)(2,1)S(1)} all-gather(bf16[128,256]{1,0:T(8,128)(2,1)} %param.28), channel_id=1, replica_groups=mesh['dp'=8,'mp'=4] {'dp'}, dimensions={0}, use_global_device_ids=true | all-gather | bytes 589824 | tf_op jit(solution)/shard_map/all_gather | solution.py:184
  46.8 33.8 %all_gather.30 = bf16[1024,256]{1,0:T(8,128)(2,1)} all-gather(bf16[128,256]{1,0:T(8,128)(2,1)} %param.29), channel_id=1, replica_groups=mesh['dp'=8,'mp'=4] {'dp'}, dimensions={0}, use_global_device_ids=true | all-gather | bytes 589824 | tf_op jit(solution)/shard_map/all_gather | solution.py:185
  80.6 33.3 %all_gather.31 = bf16[1024,256]{1,0:T(8,128)(2,1)} all-gather(bf16[128,256]{1,0:T(8,128)(2,1)S(1)} %copy-done.69), channel_id=1, replica_groups=mesh['dp'=8,'mp'=4] {'dp'}, dimensions={0}, use_global_device_ids=true | all-gather | bytes 589824 | tf_op jit(solution)/shard_map/all_gather | solution.py:186
  113.9 28.1 %all_gather.64 = bf16[256,1024]{1,0:T(8,128)(2,1)} all-gather(bf16[256,128]{1,0:T(8,128)(2,1)S(1)} %copy-done.70), channel_id=1, replica_groups=mesh['dp'=8,'mp'=4] {'dp'}, dimensions={1}, use_global_device_ids=true | all-gather | bytes 589824 | tf_op jit(solution)/shard_map/all_gather | solution.py:188
  142.0 3.3 fusion.166
  151.3 15.0 %while.54 = (s32[]{:T(128)}, bf16[2,4,512,64]{2,3,1,0:T(8,128)(2,1)S(1)}, f32[2,4,512]{2,1,0:T(4,128)S(1)}, s32[2,512]{1,0:T(2,128)S(1)}, s32[1,1024]{1,0:T(1,12...) while((s32[]{:T(128)}, ...), condition=%wide.region_3.4_spmd, body=%wide.region_0.3_spmd.sunk | while | flops 562558976 | bytes 31271056 | solution.py:90
  171.5 3.3 fusion.151
  181.0 15.0 %while.55 = (s32[]{:T(128)}, bf16[2,4,512,64]{2,3,1,0:T(8,128)(2,1)S(1)}, f32[2,4,512]{2,1,0:T(4,128)S(1)}, s32[2,512]{1,0:T(2,128)S(1)}, s32[1,1024]{1,0:T(1,12...) while((s32[]{:T(128)}, ...), condition=%wide.region_13.14_spmd, body=%wide.region_10.13_spmd.sunk | while | flops 562558976 | bytes 31271056 | solution.py:90
  201.0 13.9 %reduce-scatter.25.cloned.1.call-done = f32[256,1024]{1,0:T(8,128)} async-done(((f32[1024,1024]{1,0:T(8,128)}), f32[256,1024]{1,0:T(8,128)}) %reduce-scatter.25.cloned.1.call-update) | async-done | bytes 1048592 | tf_op jit(solution)/shard_map/reduce_scatter | solution.py:220
  214.8 47.1 %reduce-scatter.29.cloned.1.call-done = f32[256,1024]{1,0:T(8,128)} async-done(((f32[1024,1024]{1,0:T(8,128)}), f32[256,1024]{1,0:T(8,128)}) %reduce-scatter.29.cloned.1.call-update) | async-done | bytes 1048592 | tf_op jit(solution)/shard_map/reduce_scatter | solution.py:220
  268.3 20.1 %all-gather.19.cloned.1.call-done = bf16[1024,1024]{1,0:T(8,128)(2,1)} async-done(((bf16[256,1024]{1,0:T(8,128)(2,1)}), bf16[1024,1024]{1,0:T(8,128)(2,1)}) %all-gather.19.cloned.1.call-update) | async-done | bytes 2097168 | tf_op jit(solution)/shard_map/all_gather | solution.py:226
  288.4 6.5 fusion.210
  294.9 18.0 %all-gather.13.cloned.1.call-done = bf16[1024,1024]{1,0:T(8,128)(2,1)} async-done(((bf16[256,1024]{1,0:T(8,128)(2,1)}), bf16[1024,1024]{1,0:T(8,128)(2,1)}) %all-gather.13.cloned.1.call-update) | async-done | bytes 2097168 | tf_op jit(solution)/shard_map/all_gather | solution.py:226
  312.8 24.0 %multiply_convert_fusion.3 = (bf16[1024,1024]{1,0:T(8,128)(2,1)}, f32[1024,1024]{1,0:T(8,128)}, bf16[1024,1024]{1,0:T(8,128)(2,1)}, f32[1024,1024]{1,0:T(8,128)}, f32[1024,1024]{1,0:T(8,128)}) fusion(f32[1024]{0:T(1024)S(1)} %dynamic_slice.50, f32[1024,1024]{1,0:T(8,128)} %fusion.210, bf16[1024,1024]{1,0:T(8,128)(2,1)} %all-gather.13.cloned.1.call-done, ...), kind=kOutput, calls=%fused_computation.121 | convolution fusion | flops 2285895680 | bytes 25169920 | tf_op jit(solution)/shard_map/dot_general | solution.py:13
  336.8 28.6 %all-gather.17.cloned.1.call-done = bf16[1024,1024]{1,0:T(8,128)(2,1)} async-done(((bf16[1024,128]{1,0:T(8,128)(2,1)}), bf16[1024,1024]{1,0:T(8,128)(2,1)}) %all-gather.17.cloned.1.call-update) | async-done | bytes 2097168 | tf_op jit(solution)/shard_map/all_gather | solution.py:189
  365.5 6.5 fusion.208
  372.0 6.8 fusion.211
  379.1 35.6 %reduce-scatter.27.cloned.1.call-done = f32[256,1024]{1,0:T(8,128)} async-done(((f32[1024,1024]{1,0:T(8,128)}), f32[256,1024]{1,0:T(8,128)}) %reduce-scatter.27.cloned.1.call-update) | async-done | bytes 1048592 | tf_op jit(solution)/shard_map/reduce_scatter | solution.py:231
  414.7 47.1 %reduce-scatter.31.cloned.1.call-done = f32[256,1024]{1,0:T(8,128)} async-done(((f32[1024,1024]{1,0:T(8,128)}), f32[256,1024]{1,0:T(8,128)}) %reduce-scatter.31.cloned.1.call-update) | async-done | bytes 1048592 | tf_op jit(solution)/shard_map/reduce_scatter | solution.py:231
  472.9 20.5 %all-gather.25.cloned.1.call-done = bf16[1024,1024]{1,0:T(8,128)(2,1)} async-done(((bf16[256,1024]{1,0:T(8,128)(2,1)}), bf16[1024,1024]{1,0:T(8,128)(2,1)}) %all-gather.25.cloned.1.call-update) | async-done | bytes 2097168 | tf_op jit(solution)/shard_map/all_gather | solution.py:284
  493.4 6.5 fusion.215
  500.0 17.5 %all-gather.21.cloned.1.call-done = bf16[1024,1024]{1,0:T(8,128)(2,1)} async-done(((bf16[256,1024]{1,0:T(8,128)(2,1)}), bf16[1024,1024]{1,0:T(8,128)(2,1)}) %all-gather.21.cloned.1.call-update) | async-done | bytes 2097168 | tf_op jit(solution)/shard_map/all_gather | solution.py:284
  517.5 14.0 %convert_reduce_fusion.1 = (f32[1024]{0:T(1024)}, bf16[1024,1024]{1,0:T(8,128)(2,1)S(1)}, f32[1024]{0:T(1024)}, bf16[1024,1024]{1,0:T(8,128)(2,1)}) fusion(f32[1024,1024]{1,0:T(8,128)} %get-tuple-element.556, f32[1024,1024]{1,0:T(8,128)} %get-tuple-element.597, f32[1024]{0:T(1024)S(1)} %dynamic_slice.50, f32[1024,1024]{1,0:T(8,128)} %fusion.215, ...), kind=kOutput, calls=%fused_computation.101 | convolution fusion | flops 2183133184 | bytes 29372416 | tf_op jit(solution)/shard_map/dot_general | solution.py:23
  532.8 4.3 fusion.212
  537.2 6.6 fusion.216
  544.3 37.5 %reduce-scatter.33.cloned.1.call-done = f32[256,1024]{1,0:T(8,128)} async-done(((f32[1024,1024]{1,0:T(8,128)}), f32[256,1024]{1,0:T(8,128)}) %reduce-scatter.33.cloned.1.call-update) | async-done | bytes 1048592 | tf_op jit(solution)/shard_map/reduce_scatter | solution.py:289
  581.8 3.2 multiply_reduce_fusion.3
  585.0 44.1 %reduce-scatter.37.cloned.1.call-done = f32[256,1024]{1,0:T(8,128)} async-done(((f32[1024,1024]{1,0:T(8,128)}), f32[256,1024]{1,0:T(8,128)}) %reduce-scatter.37.cloned.1.call-update) | async-done | bytes 1048592 | tf_op jit(solution)/shard_map/reduce_scatter | solution.py:289
  629.1 3.3 fusion.197
  636.3 4.8 fusion.221
  646.5 4.8 fusion.220
  651.3 3.9 add_convert_fusion.1
  657.8 3.2 convolution_convert_fusion
  666.0 25.2 %while.57 = (s32[]{:T(128)}, f32[4,1024,64]{1,2,0:T(8,128)S(1)}, f32[4,1024,64]{1,2,0:T(8,128)}, bf16[2,4,512,64]{2,3,1,0:T(8,128)(2,1)}, s32[2,512]{1,0:T(2,128...) while((s32[]{:T(128)}, f32[4,1024,64]{1,2,0:T(8,128)S(1)}, ...), condition=%wide.region_36.37_spmd.clone, body=%wide.region_34.36_spmd.clone.sunk | while | flops 1375598592 | bytes 89196888 | solution.py:142
  670.8 3.2 multiply_reduce_fusion.15
  683.2 3.2 multiply_reduce_fusion.15
  697.4 3.3 convolution_convert_fusion.1
  705.7 25.1 %while.56 = (s32[]{:T(128)}, f32[4,1024,64]{1,2,0:T(8,128)S(1)}, f32[4,1024,64]{1,2,0:T(8,128)}, bf16[2,4,512,64]{2,3,1,0:T(8,128)(2,1)}, s32[2,512]{1,0:T(2,128...) while((s32[]{:T(128)}, f32[4,1024,64]{1,2,0:T(8,128)S(1)}, ...), condition=%wide.region_27.28_spmd.clone, body=%wide.region_25.27_spmd.clone.sunk | while | flops 1375598592 | bytes 89196888 | solution.py:142
  710.4 3.2 multiply_reduce_fusion.14
  722.9 3.2 multiply_reduce_fusion.14
  765.9 57.5 %reduce-scatter.41.cloned.1.call-done = bf16[128,1024]{1,0:T(8,128)(2,1)} async-done(((bf16[1024,1024]{1,0:T(8,128)(2,1)}), bf16[128,1024]{1,0:T(8,128)(2,1)}) %reduce-scatter.41.cloned.1.call-update) | async-done | bytes 262160 | tf_op jit(solution)/shard_map/reduce_scatter | solution.py:359
  826.2 41.0 %all-reduce = (f32[1024]{0:T(1024)}, f32[1024]{0:T(1024)}, f32[1024]{0:T(1024)}, f32[4096]{0:T(1024)}, f32[1024]{0:T(1024)}, /*index=5*/f32[1024]{0:T(1024)}, f32[1024]{0:T(1024)}, f32[1024]{0:T(1024)}, f32[1024]{0:T(1024)}) all-reduce(f32[1024]{0:T(1024)S(1)} %dynamic_update_slice.29, ...), channel_id=1, replica_groups=mesh['dp'=8,'mp'=4] {'dp','mp'}, use_global_device_ids=true, to_apply=%region_46.47 | all-reduce | flops 12288 | bytes 98304 | tf_op jit(solution)/shard_map/psum | solution.py:378
  867.2 20.3 %reduce-scatter.49.cloned.1.call-done = bf16[128,256]{1,0:T(8,128)(2,1)} async-done(((bf16[1024,256]{1,0:T(8,128)(2,1)}), bf16[128,256]{1,0:T(8,128)(2,1)}) %reduce-scatter.49.cloned.1.call-update) | async-done | bytes 65552
  889.1 63.1 %reduce-scatter.47.cloned.1.call-done = bf16[128,256]{1,0:T(8,128)(2,1)} async-done(((bf16[1024,256]{1,0:T(8,128)(2,1)}), bf16[128,256]{1,0:T(8,128)(2,1)}) %reduce-scatter.47.cloned.1.call-update) | async-done | bytes 65552
  954.0 62.5 %reduce-scatter.43.cloned.1.call-done = bf16[128,256]{1,0:T(8,128)(2,1)} async-done(((bf16[1024,256]{1,0:T(8,128)(2,1)}), bf16[128,256]{1,0:T(8,128)(2,1)}) %reduce-scatter.43.cloned.1.call-update) | async-done | bytes 65552
  1018.2 63.0 %reduce-scatter.45.cloned.1.call-done = bf16[128,256]{1,0:T(8,128)(2,1)} async-done(((bf16[1024,256]{1,0:T(8,128)(2,1)}), bf16[128,256]{1,0:T(8,128)(2,1)}) %reduce-scatter.45.cloned.1.call-update) | async-done | bytes 65552
  1083.0 31.2 %reduce-scatter.35.cloned.1.call-done = bf16[256,1024]{1,0:T(8,128)(2,1)} async-done(((bf16[1024,1024]{1,0:T(8,128)(2,1)}), bf16[256,1024]{1,0:T(8,128)(2,1)}) %reduce-scatter.35.cloned.1.call-update) | async-done | bytes 524304 | tf_op jit(solution)/shard_map/reduce_scatter | solution.py:304
  1115.4 33.4 %reduce-scatter.39.cloned.1.call-done = bf16[256,1024]{1,0:T(8,128)(2,1)} async-done(((bf16[1024,1024]{1,0:T(8,128)(2,1)}), bf16[256,1024]{1,0:T(8,128)(2,1)}) %reduce-scatter.39.cloned.1.call-update) | async-done | bytes 524304 | tf_op jit(solution)/shard_map/reduce_scatter | solution.py:304
  (452 shorter events, 188.9 us)
Async XLA Ops:
  8.0 72.5 %copy-start.69 = (bf16[128,256]{1,0:T(8,128)(2,1)S(1)}, bf16[128,256]{1,0:T(8,128)(2,1)}, u32[]{:S(2)}) copy-start(bf16[128,256]{1,0:T(8,128)(2,1)} %param.30) | copy-start | bytes 196612
  8.0 105.8 %copy-start.70 = (bf16[256,128]{1,0:T(8,128)(2,1)S(1)}, bf16[256,128]{1,0:T(8,128)(2,1)}, u32[]{:S(2)}) copy-start(bf16[256,128]{1,0:T(8,128)(2,1)} %param.31) | copy-start | bytes 196612
  8.0 134.0 %all-gather.29.cloned.1.call-start = ((), (), s32[]{:S(2)}) async-start(), calls=%async_computation.31 | async-start | bytes 2621440 | tf_op jit(solution)/shard_map/all_gather | solution.py:208
  10.3 160.5 %all-gather.31.cloned.1.call-start = ((), (), s32[]{:S(2)}) async-start(), calls=%async_computation.32 | async-start | bytes 2621440 | tf_op jit(solution)/shard_map/all_gather | solution.py:208
  11.1 203.7 %reduce-scatter.25.cloned.1.call-start = ((), (), s32[]{:S(2)}) async-start(), calls=%async_computation.14 | async-start | bytes 5242880 | tf_op jit(solution)/shard_map/reduce_scatter | solution.py:220
  46.8 100.0 %copy-start.32 = (bf16[1024,256]{1,0:T(8,128)(2,1)}, bf16[1024,256]{1,0:T(8,128)(2,1)S(1)}, u32[]{:S(2)}) copy-start(bf16[1024,256]{1,0:T(8,128)(2,1)S(1)} %all_gather.29) | copy-start | bytes 1572868
  151.3 16.5 %copy-start.35 = (bf16[256,1024]{1,0:T(8,128)(2,1)S(1)}, bf16[256,1024]{1,0:T(8,128)(2,1)}, u32[]{:S(2)}) copy-start(bf16[256,1024]{1,0:T(8,128)(2,1)} %all_gather.64) | copy-start | bytes 1572868
  170.5 91.4 %reduce-scatter.29.cloned.1.call-start = ((), (), s32[]{:S(2)}) async-start(), calls=%async_computation.19 | async-start | bytes 5242880 | tf_op jit(solution)/shard_map/reduce_scatter | solution.py:220
  181.0 16.5 %copy-start.36 = (bf16[256,1024]{1,0:T(8,128)(2,1)S(1)}, bf16[256,1024]{1,0:T(8,128)(2,1)}, u32[]{:S(2)}) copy-start(bf16[256,1024]{1,0:T(8,128)(2,1)} %all_gather.64) | copy-start | bytes 1572868
  200.3 61.7 %copy-start.51 = (bf16[2,256,1024]{2,1,0:T(8,128)(2,1)S(1)}, bf16[2,256,1024]{2,1,0:T(8,128)(2,1)}, u32[]{:S(2)}) copy-start(bf16[2,256,1024]{2,1,0:T(8,128)(2,1)} %param.26) | copy-start | bytes 3145732
  200.3 61.7 %copy-start.86 = (f32[1024]{0:T(1024)S(1)}, f32[1024]{0:T(1024)}, u32[]{:S(2)}) copy-start(f32[1024]{0:T(1024)} %param.36) | copy-start | bytes 12292
  200.3 64.1 %copy-start.68 = (f32[1024]{0:T(1024)S(1)}, f32[1024]{0:T(1024)}, u32[]{:S(2)}) copy-start(f32[1024]{0:T(1024)} %param.39) | copy-start | bytes 12292
  200.3 64.1 %copy-start.80 = (f32[1024]{0:T(1024)S(1)}, f32[1024]{0:T(1024)}, u32[]{:S(2)}) copy-start(f32[1024]{0:T(1024)} %param.40) | copy-start | bytes 12292
  200.3 68.0 %all-gather.15.cloned.1.call-start = ((), (), s32[]{:S(2)}) async-start(), calls=%async_computation.16 | async-start | bytes 2359296 | tf_op jit(solution)/shard_map/all_gather | solution.py:187
  200.9 87.5 %all-gather.19.cloned.1.call-start = ((), (), s32[]{:S(2)}) async-start(), calls=%async_computation.20 | async-start | bytes 2621440 | tf_op jit(solution)/shard_map/all_gather | solution.py:226
  265.8 47.0 %all-gather.13.cloned.1.call-start = ((), (), s32[]{:S(2)}) async-start(), calls=%async_computation.15 | async-start | bytes 2621440 | tf_op jit(solution)/shard_map/all_gather | solution.py:226
  266.4 99.1 %all-gather.17.cloned.1.call-start = ((), (), s32[]{:S(2)}) async-start(), calls=%async_computation.17 | async-start | bytes 2359296 | tf_op jit(solution)/shard_map/all_gather | solution.py:189
  267.1 147.6 %reduce-scatter.27.cloned.1.call-start = ((), (), s32[]{:S(2)}) async-start(), calls=%async_computation.18 | async-start | bytes 5242880 | tf_op jit(solution)/shard_map/reduce_scatter | solution.py:231
  372.0 89.8 %reduce-scatter.31.cloned.1.call-start = ((), (), s32[]{:S(2)}) async-start(), calls=%async_computation.21 | async-start | bytes 5242880 | tf_op jit(solution)/shard_map/reduce_scatter | solution.py:231
  378.8 83.0 %copy-start.87 = (f32[1024]{0:T(1024)S(1)}, f32[1024]{0:T(1024)}, u32[]{:S(2)}) copy-start(f32[1024]{0:T(1024)} %param.38) | copy-start | bytes 12292
  378.9 85.6 %copy-start.20 = (bf16[2,256,1024]{2,1,0:T(8,128)(2,1)S(1)}, bf16[2,256,1024]{2,1,0:T(8,128)(2,1)}, u32[]{:S(2)}) copy-start(bf16[2,256,1024]{2,1,0:T(8,128)(2,1)} %param.43) | copy-start | bytes 3145732
  378.9 85.6 %copy-start.71 = (f32[1024]{0:T(1024)S(1)}, f32[1024]{0:T(1024)}, u32[]{:S(2)}) copy-start(f32[1024]{0:T(1024)} %param.41) | copy-start | bytes 12292
  378.9 114.6 %all-gather.25.cloned.1.call-start = ((), (), s32[]{:S(2)}) async-start(), calls=%async_computation.26 | async-start | bytes 2621440 | tf_op jit(solution)/shard_map/all_gather | solution.py:284
  470.7 46.8 %all-gather.21.cloned.1.call-start = ((), (), s32[]{:S(2)}) async-start(), calls=%async_computation.22 | async-start | bytes 2621440 | tf_op jit(solution)/shard_map/all_gather | solution.py:284
  472.9 109.0 %reduce-scatter.33.cloned.1.call-start = ((), (), s32[]{:S(2)}) async-start(), calls=%async_computation.23 | async-start | bytes 5242880 | tf_op jit(solution)/shard_map/reduce_scatter | solution.py:289
  517.5 15.3 %copy-start.89 = (bf16[1024,1024]{1,0:T(8,128)(2,1)S(1)}, bf16[1024,1024]{1,0:T(8,128)(2,1)}, u32[]{:S(2)}) copy-start(bf16[1024,1024]{1,0:T(8,128)(2,1)} %all-gather.15.cloned.1.call-done) | copy-start | bytes 6291460
  537.2 91.9 %reduce-scatter.37.cloned.1.call-start = ((), (), s32[]{:S(2)}) async-start(), calls=%async_computation.27 | async-start | bytes 5242880 | tf_op jit(solution)/shard_map/reduce_scatter | solution.py:289
  543.8 38.0 %copy-start.25 = (f32[256,1024]{1,0:T(8,128)S(1)}, f32[256,1024]{1,0:T(8,128)}, u32[]{:S(2)}) copy-start(f32[256,1024]{1,0:T(8,128)} %get-tuple-element.577) | copy-start | bytes 3145732
  543.9 113.9 %all-gather.27.cloned.1.call-start = ((), (), s32[]{:S(2)}) async-start(), calls=%async_computation.28 | async-start | bytes 2621440 | tf_op jit(solution)/shard_map/all_gather | solution.py:295
  635.2 56.0 %all-gather.23.cloned.1.call-start = ((), (), s32[]{:S(2)}) async-start(), calls=%async_computation.24 | async-start | bytes 2621440 | tf_op jit(solution)/shard_map/all_gather | solution.py:295
  636.2 127.7 %reduce-scatter.51.cloned.1.call-start = ((), (), s32[]{:S(2)}) async-start(), calls=%async_computation.37 | async-start | bytes 2359296
  646.3 177.1 %reduce-scatter.41.cloned.1.call-start = ((), (), s32[]{:S(2)}) async-start(), calls=%async_computation.30 | async-start | bytes 2359296 | tf_op jit(solution)/shard_map/reduce_scatter | solution.py:359
  655.3 232.2 %reduce-scatter.49.cloned.1.call-start = ((), (), s32[]{:S(2)}) async-start(), calls=%async_computation.36 | async-start | bytes 589824
  730.9 221.4 %reduce-scatter.47.cloned.1.call-start = ((), (), s32[]{:S(2)}) async-start(), calls=%async_computation.35 | async-start | bytes 589824
  740.0 276.5 %reduce-scatter.43.cloned.1.call-start = ((), (), s32[]{:S(2)}) async-start(), calls=%async_computation.33 | async-start | bytes 589824
  747.6 333.7 %reduce-scatter.45.cloned.1.call-start = ((), (), s32[]{:S(2)}) async-start(), calls=%async_computation.34 | async-start | bytes 589824
  752.3 361.9 %reduce-scatter.35.cloned.1.call-start = ((), (), s32[]{:S(2)}) async-start(), calls=%async_computation.25 | async-start | bytes 2621440 | tf_op jit(solution)/shard_map/reduce_scatter | solution.py:304
  757.2 391.6 %reduce-scatter.39.cloned.1.call-start = ((), (), s32[]{:S(2)}) async-start(), calls=%async_computation.29 | async-start | bytes 2621440 | tf_op jit(solution)/shard_map/reduce_scatter | solution.py:304
  760.9 64.3 %copy-start.78 = (f32[1024]{0:T(1024)S(1)}, f32[1024]{0:T(1024)}, u32[]{:S(2)}) copy-start(f32[1024]{0:T(1024)} %get-tuple-element.591) | copy-start | bytes 12292
  760.9 64.3 %copy-start.82 = (f32[1024]{0:T(1024)S(1)}, f32[1024]{0:T(1024)}, u32[]{:S(2)}) copy-start(f32[1024]{0:T(1024)} %get-tuple-element.436) | copy-start | bytes 12292
  761.0 64.3 %copy-start.77 = (f32[1024]{0:T(1024)S(1)}, f32[1024]{0:T(1024)}, u32[]{:S(2)}) copy-start(f32[1024]{0:T(1024)} %get-tuple-element.588) | copy-start | bytes 12292
  761.0 64.3 %copy-start.81 = (f32[1024]{0:T(1024)S(1)}, f32[1024]{0:T(1024)}, u32[]{:S(2)}) copy-start(f32[1024]{0:T(1024)} %get-tuple-element.447) | copy-start | bytes 12292
  761.0 64.3 %copy-start.76 = (f32[1024]{0:T(1024)S(1)}, f32[1024]{0:T(1024)}, u32[]{:S(2)}) copy-start(f32[1024]{0:T(1024)} %get-tuple-element.545) | copy-start | bytes 12292
  761.0 64.3 %copy-start.79 = (f32[1024]{0:T(1024)S(1)}, f32[1024]{0:T(1024)}, u32[]{:S(2)}) copy-start(f32[1024]{0:T(1024)} %get-tuple-element.543) | copy-start | bytes 12292
  761.0 64.3 %copy-start.42 = (bf16[2,4,512,64]{2,3,1,0:T(8,128)(2,1)S(1)}, bf16[2,4,512,64]{2,3,1,0:T(8,128)(2,1)}, u32[]{:S(2)}) copy-start(bf16[2,4,512,64]{2,3,1,0:T(8,128)(2,1)} %get-tuple-element.228) | copy-start | bytes 1572868
  761.0 64.4 %copy-start.45 = (bf16[2,4,512,64]{2,3,1,0:T(8,128)(2,1)S(1)}, bf16[2,4,512,64]{2,3,1,0:T(8,128)(2,1)}, u32[]{:S(2)}) copy-start(bf16[2,4,512,64]{2,3,1,0:T(8,128)(2,1)} %get-tuple-element.224) | copy-start | bytes 1572868
  761.1 353.1 %copy-start.23 = (f32[256,1024]{1,0:T(8,128)S(1)}, f32[256,1024]{1,0:T(8,128)}, u32[]{:S(2)}) copy-start(f32[256,1024]{1,0:T(8,128)} %copy-done.22) | copy-start | bytes 3145732
  761.3 387.5 %copy-start.19 = (f32[256,1024]{1,0:T(8,128)S(1)}, f32[256,1024]{1,0:T(8,128)}, u32[]{:S(2)}) copy-start(f32[256,1024]{1,0:T(8,128)} %copy-done.18) | copy-start | bytes 3145732
  (84 other events, 306.7 us)
Sparse Core Ops, SparseCore 0:
  11.0 25.2 all-gather.28
  38.5 22.5 all-gather.30
  170.7 44.1 reduce-scatter.24
  217.4 44.5 reduce-scatter.28
  470.8 22.5 all-gather.24
  494.9 22.5 all-gather.20
  537.3 44.4 reduce-scatter.32
  584.5 44.5 reduce-scatter.36
Sparse Core Ops, SparseCore 1:
  202.9 48.7 all-gather.14
  265.9 22.4 all-gather.18
  290.4 22.4 all-gather.12
  314.9 50.5 all-gather.16
  372.1 42.6 reduce-scatter.26
  417.4 44.4 reduce-scatter.30
  635.3 22.4 all-gather.26
  659.2 22.4 all-gather.22
  685.1 68.0 reduce-scatter.50
  756.7 66.7 reduce-scatter.40
  826.6 60.8 reduce-scatter.48
  891.2 61.0 reduce-scatter.46
  955.5 61.0 reduce-scatter.42
  1020.2 61.0 reduce-scatter.44
  1083.8 30.3 reduce-scatter.34
  1117.5 31.3 reduce-scatter.38
where the time goes:
time: 1170 us; the launch traced here: 1160 us
  waiting for transfers between devices  666 us (57%)
  matrix products  198 us (17%)
  blocking collectives  169 us (14%)
  other arithmetic  58.2 us (5%)
  local copies, waits for them, and re-layouts  45.8 us (4%)
  between operations  17.8 us (2%)
    unnamed x29, waiting for transfers between devices  212 us
    reduce_scatter x2, waiting for transfers between devices, on_device(): lax.psum_scatter(matmul(forward_active, forward_down_all), 'mp', scatter_...  82.7 us
    reduce_scatter x2, waiting for transfers between devices, on_device(): lax.psum_scatter(outer_cols(grad_hidden, up_all), 'mp', scatter_dimension...  81.6 us
    dot_general x12, matrix products, matmul(): return jnp.dot(left_mat, right_mat, preferred_element_type=jnp.float32)  64.7 us
    reduce_scatter x2, waiting for transfers between devices, on_device(): lax.psum_scatter((outer_cols(grad_queries, query_all) + outer_cols(grad_k...  64.6 us
    reduce_scatter x2, waiting for transfers between devices, on_device(): lax.psum_scatter(matmul(forward_context, forward_out_all), 'mp', scatter_...  61 us
    reduce_scatter x1, waiting for transfers between devices, on_device(): lax.psum_scatter(weight_sums[3].astype(jnp.bfloat16), 'dp', scatter_dimen...  57.5 us
    dot_general x12, matrix products, outer_cols(): lax.dot_general(left_mat, right_mat, (((1,), (1,)), ((), ())), preferred_...  46.3 us
  transfers between devices with their start and end apart: 24, of which 19 were waited for; matrix products, arithmetic and copies ran while one was open for 22% of the time, Pallas kernels for 0%

commit v1 on v0

v1 whole, which is shorter than its diff:
```python
import functools

import jax
import jax.numpy as jnp
from jax import lax
from jax.sharding import PartitionSpec as P

HDIM = 64


epsilon = 1e-06


def matmul(left_mat, right_mat):
    return jnp.dot(left_mat, right_mat, preferred_element_type=jnp.float32)


def inner_rows(left_mat, right_mat):
    return lax.dot_general(
        left_mat, right_mat, (((0,), (0,)), ((), ())), preferred_element_type=jnp.float32
    )


def outer_cols(left_mat, right_mat):
    return lax.dot_general(
        left_mat, right_mat, (((1,), (1,)), ((), ())), preferred_element_type=jnp.float32
    )


def norm_forward(residual, scale_vec, shift_vec):
    mean_val = jnp.mean(residual, axis=-1, keepdims=True)
    centred = residual - mean_val
    inverse = lax.rsqrt(jnp.mean(centred * centred, axis=-1, keepdims=True) + epsilon)
    normed = centred * inverse
    return (normed * scale_vec + shift_vec, normed, inverse)


def norm_backward(incoming, normed, inverse, scale_vec):
    scaled = incoming * scale_vec
    centre_term = jnp.mean(scaled, axis=-1, keepdims=True)
    slope_term = jnp.mean(scaled * normed, axis=-1, keepdims=True)
    return (
        inverse * (scaled - centre_term - normed * slope_term),
        jnp.sum(incoming * normed, axis=0),
        jnp.sum(incoming, axis=0),
    )


def gelu_exact(values_in):
    return jax.nn.gelu(values_in, approximate=False)


def head_major(matrix, head_count):
    return matrix.reshape(matrix.shape[0], head_count, HDIM).transpose(1, 0, 2)


def head_blocks(matrix, head_count, block_rows):
    row_count = matrix.shape[0]
    return (
        head_major(matrix, head_count)
        .reshape(head_count, row_count // block_rows, block_rows, HDIM)
        .transpose(1, 0, 2, 3)
    )


def score_block(query_block, key_heads, query_segs, key_segs):
    raw_scores = jnp.einsum(
        "hqd,hkd->hqk", query_block, key_heads, preferred_element_type=jnp.float32
    )
    same_doc = (query_segs[:, None] == key_segs[None, :])[None]
    return jnp.where(same_doc, raw_scores * HDIM ** (-0.5), -1000000000.0)


def attention_forward(queries, key_rows, value_rows, seg_row, head_count):
    row_count = queries.shape[0]
    block_rows = min(512, row_count)
    key_heads = head_major(key_rows, head_count)
    value_heads = head_major(value_rows, head_count)

    def one_block(pieces):
        query_block, query_segs = pieces
        scores = score_block(query_block, key_heads, query_segs, seg_row)
        top_val = jnp.max(scores, axis=-1, keepdims=True)
        exponent = jnp.exp(scores - top_val)
        totals = jnp.sum(exponent, axis=-1, keepdims=True)
        probabilities = (exponent / totals).astype(jnp.bfloat16)
        context = jnp.einsum(
            "hqk,hkd->hqd", probabilities, value_heads, preferred_element_type=jnp.float32
        )
        return (context, (top_val + jnp.log(totals))[..., 0])

    context, log_totals = lax.map(
        one_block, (head_blocks(queries, head_count, block_rows), seg_row.reshape(-1, block_rows))
    )
    return (context.transpose(0, 2, 1, 3).reshape(row_count, head_count * HDIM), log_totals)


def attention_backward(
    queries, key_rows, value_rows, seg_row, log_totals, grad_context, head_count
):
    row_count = queries.shape[0]
    block_rows = min(512, row_count)
    key_heads = head_major(key_rows, head_count)
    value_heads = head_major(value_rows, head_count)
    scale_val = HDIM ** (-0.5)

    def one_block(sum_pair, pieces):
        query_block, grad_block, query_segs, block_lse = pieces
        scores = score_block(query_block, key_heads, query_segs, seg_row)
        probabilities = jnp.exp(scores - block_lse[..., None])
        grad_probs = jnp.einsum(
            "hqd,hkd->hqk", grad_block, value_heads, preferred_element_type=jnp.float32
        )
        grad_scores = (
            probabilities
            * (grad_probs - jnp.sum(grad_probs * probabilities, axis=-1, keepdims=True))
        ).astype(jnp.bfloat16)
        grad_query = (
            jnp.einsum("hqk,hkd->hqd", grad_scores, key_heads, preferred_element_type=jnp.float32)
            * scale_val
        )
        key_sum = (
            sum_pair[0]
            + jnp.einsum(
                "hqk,hqd->hkd", grad_scores, query_block, preferred_element_type=jnp.float32
            )
            * scale_val
        )
        value_sum = sum_pair[1] + jnp.einsum(
            "hqk,hqd->hkd",
            probabilities.astype(jnp.bfloat16),
            grad_block,
            preferred_element_type=jnp.float32,
        )
        return ((key_sum, value_sum), grad_query)

    zero_acc = jnp.zeros((head_count, row_count, HDIM), jnp.float32)
    pieces = (
        head_blocks(queries, head_count, block_rows),
        head_blocks(grad_context, head_count, block_rows),
        seg_row.reshape(-1, block_rows),
        log_totals,
    )
    (key_sum, value_sum), grad_query = lax.scan(one_block, (zero_acc, zero_acc), pieces)
    grad_query = grad_query.transpose(0, 2, 1, 3).reshape(row_count, head_count * HDIM)
    key_sum = key_sum.transpose(1, 0, 2).reshape(row_count, head_count * HDIM)
    value_sum = value_sum.transpose(1, 0, 2).reshape(row_count, head_count * HDIM)
    return (
        grad_query.astype(jnp.bfloat16),
        key_sum.astype(jnp.bfloat16),
        value_sum.astype(jnp.bfloat16),
    )


def steps_of(count):
    bit, found = count // 2, []
    while bit:
        found.append(bit)
        bit //= 2
    return found


def swap(block, axis_name, count, bit):
    return lax.ppermute(block, axis_name, [(i, i ^ bit) for i in range(count)])


def rank_order(count):
    order = [0]
    for bit in steps_of(count):
        order = order + [item ^ bit for item in order]
    return order


def gather_rows(block, count):
    for bit in steps_of(count):
        block = jnp.concatenate([block, swap(block, "mp", count, bit)], axis=0)
    return block


def scatter_rows(product_of, rows, count):
    half = rows // 2
    kept = None
    for bit in reversed(steps_of(count)):
        if kept is None:
            sent = product_of(half, rows).astype(jnp.bfloat16)
            came = swap(sent, "mp", count, bit)
            kept = product_of(0, half)
        else:
            sent = kept[half:].astype(jnp.bfloat16)
            came = swap(sent, "mp", count, bit)
            kept = kept[:half]
        kept = kept + came.astype(jnp.float32)
        half //= 2
    return kept


def gather_shards(block, count):
    rank = lax.axis_index("dp")
    rows = block.shape[0]
    width = block.shape[1]
    held = block.reshape(1, rows, width)
    for bit in steps_of(count):
        came = swap(held, "dp", count, bit)
        low = (rank & bit) == 0
        first = jnp.where(low, held, came)
        second = jnp.where(low, came, held)
        held = jnp.stack([first, second], axis=1).reshape(-1, rows, width)
    return held.reshape(count * rows, width)


def reduce_shards(total, count):
    rank = lax.axis_index("dp")
    rows = total.shape[0] // count
    held = total.reshape(count, rows, total.shape[1])
    for bit in reversed(steps_of(count)):
        pairs = held.reshape(held.shape[0] // 2, 2, rows, held.shape[2])
        low = (rank & bit) == 0
        sent = jnp.where(low, pairs[:, 1], pairs[:, 0])
        kept = jnp.where(low, pairs[:, 0], pairs[:, 1])
        came = swap(sent.astype(jnp.bfloat16), "dp", count, bit)
        held = kept.astype(jnp.float32) + came.astype(jnp.float32)
    return held[0]


def add_everywhere(vector, mp_count, dp_count):
    for axis_name, count in (("mp", mp_count), ("dp", dp_count)):
        for bit in steps_of(count):
            vector = vector + swap(vector, axis_name, count, bit)
    return vector


def gelu_pair(hidden):
    phi_cap = 0.5 * (1.0 + lax.erf(hidden * 0.7071067811865476))
    density = jnp.exp(-0.5 * hidden * hidden) * 0.3989422804014327
    return (
        (hidden * phi_cap).astype(jnp.bfloat16),
        (phi_cap + hidden * density).astype(jnp.bfloat16),
    )


def on_device(
    dp_count,
    mp_count,
    inputs,
    segments,
    query_weight,
    key_weight,
    value_weight,
    out_weight,
    up_weight,
    down_weight,
    query_bias,
    value_bias,
    out_bias,
    up_bias,
    down_bias,
    first_gain,
    first_shift,
    second_gain,
    second_shift,
    cotangent,
):
    micro_count = inputs.shape[0]
    head_cols = query_weight.shape[1]
    unit_cols = up_weight.shape[1]
    head_count = head_cols // HDIM
    mp_rank = lax.axis_index("mp")
    own_rows = inputs.shape[1]
    rows = own_rows * mp_count
    query_bias_own = lax.dynamic_slice_in_dim(query_bias, mp_rank * head_cols, head_cols)
    value_bias_own = lax.dynamic_slice_in_dim(value_bias, mp_rank * head_cols, head_cols)
    up_bias_own = lax.dynamic_slice_in_dim(up_bias, mp_rank * unit_cols, unit_cols)
    qkv_bias = jnp.concatenate([query_bias_own, jnp.zeros_like(query_bias_own), value_bias_own])
    order = [mp_rank ^ item for item in rank_order(mp_count)]

    qkv_all = gather_shards(
        jnp.concatenate([query_weight, key_weight, value_weight], axis=1), dp_count
    )
    out_t, up_all, down_t = (
        lax.all_gather(out_weight.T, "dp", axis=0, tiled=True),
        lax.all_gather(up_weight, "dp", axis=0, tiled=True),
        lax.all_gather(down_weight.T, "dp", axis=0, tiled=True),
    )

    results = []
    saved_list = []
    for micro in range(micro_count):
        own_tokens = inputs[micro]
        seg_blocks = segments[micro].reshape(mp_count, own_rows)
        seg_row = jnp.concatenate(
            [lax.dynamic_index_in_dim(seg_blocks, item, 0, keepdims=False) for item in order]
        )
        token_rows = gather_rows(own_tokens, mp_count)
        qkv = (matmul(token_rows, qkv_all) + qkv_bias).astype(jnp.bfloat16)
        queries = qkv[:, :head_cols]
        key_rows = qkv[:, head_cols : 2 * head_cols]
        value_rows = qkv[:, 2 * head_cols :]
        context, log_totals = attention_forward(queries, key_rows, value_rows, seg_row, head_count)
        context = context.astype(jnp.bfloat16)
        attention_out = scatter_rows(
            lambda low, high: outer_cols(context[low:high], out_t), rows, mp_count
        )
        first_out, first_normed, first_inverse = norm_forward(
            own_tokens.astype(jnp.float32) + attention_out + out_bias, first_gain, first_shift
        )
        first_rows = gather_rows(first_out.astype(jnp.bfloat16), mp_count)
        active, slope = lax.optimization_barrier(
            gelu_pair(matmul(first_rows, up_all) + up_bias_own)
        )
        feed_out = scatter_rows(
            lambda low, high: outer_cols(active[low:high], down_t), rows, mp_count
        )
        final_out, second_normed, second_inverse = norm_forward(
            first_out + feed_out + down_bias, second_gain, second_shift
        )
        results.append(final_out.astype(jnp.bfloat16))
        saved_list.append(
            (
                token_rows, seg_row, queries, key_rows, value_rows, log_totals, context,
                first_normed, first_inverse, first_rows, active, slope,
                second_normed, second_inverse,
            )
        )
    vector_sums = None
    input_grads = []
    pieces = []
    for micro in range(micro_count):
        (
            token_rows, seg_row, queries, key_rows, value_rows, log_totals, context,
            first_normed, first_inverse, first_rows, active, slope,
            second_normed, second_inverse,
        ) = saved_list[micro]
        incoming = cotangent[micro].astype(jnp.float32)
        grad_second, grad_second_gain, grad_second_shift = norm_backward(
            incoming, second_normed, second_inverse, second_gain
        )
        feed_rows = gather_rows(grad_second.astype(jnp.bfloat16), mp_count)
        grad_hidden = lax.optimization_barrier(
            (matmul(feed_rows, down_t) * slope.astype(jnp.float32)).astype(jnp.bfloat16)
        )
        grad_first = grad_second + scatter_rows(
            lambda low, high: outer_cols(grad_hidden[low:high], up_all), rows, mp_count
        )
        grad_resid, grad_first_gain, grad_first_shift = norm_backward(
            grad_first, first_normed, first_inverse, first_gain
        )
        attention_rows = gather_rows(grad_resid.astype(jnp.bfloat16), mp_count)
        grad_context = matmul(attention_rows, out_t).astype(jnp.bfloat16)
        grad_queries, grad_keys, grad_values = attention_backward(
            queries, key_rows, value_rows, seg_row, log_totals, grad_context, head_count
        )
        grad_qkv = jnp.concatenate([grad_queries, grad_keys, grad_values], axis=1)
        token_grad = scatter_rows(
            lambda low, high: outer_cols(grad_qkv[low:high], qkv_all), rows, mp_count
        )
        input_grads.append(grad_resid + token_grad)
        pieces.append(
            (token_rows, grad_qkv, attention_rows, context, first_rows, grad_hidden, feed_rows, active)
        )
        qkv_sums = jnp.sum(grad_qkv.astype(jnp.float32), axis=0)
        vector_terms = (
            qkv_sums[:head_cols],
            qkv_sums[2 * head_cols :],
            jnp.sum(grad_resid, axis=0),
            jnp.sum(grad_hidden.astype(jnp.float32), axis=0),
            jnp.sum(grad_second, axis=0),
            grad_first_gain,
            grad_first_shift,
            grad_second_gain,
            grad_second_shift,
        )
        vector_sums = (
            vector_terms
            if vector_sums is None
            else jax.tree.map(jnp.add, vector_sums, vector_terms)
        )

    def over_micros(left_place, right_place):
        total = inner_rows(pieces[0][left_place], pieces[0][right_place])
        for item in pieces[1:]:
            total = total + inner_rows(item[left_place], item[right_place])
        return total.astype(jnp.bfloat16)

    def scatter_sum(total):
        return lax.psum_scatter(total, "dp", scatter_dimension=0, tiled=True).astype(jnp.float32)

    ffn_sum = scatter_sum(jnp.concatenate([over_micros(6, 7), over_micros(4, 5)], axis=1))
    grad_down = ffn_sum[:, :unit_cols].T
    grad_up = ffn_sum[:, unit_cols:]
    att_sum = reduce_shards(jnp.concatenate([over_micros(0, 1), over_micros(2, 3)], axis=1), dp_count)
    grad_query = att_sum[:, :head_cols]
    grad_key = att_sum[:, head_cols : 2 * head_cols]
    grad_value = att_sum[:, 2 * head_cols : 3 * head_cols]
    grad_out = att_sum[:, 3 * head_cols :].T

    def widen(vector_part, full_size, offset):
        return lax.dynamic_update_slice_in_dim(
            jnp.zeros((full_size,), jnp.float32), vector_part, offset, 0
        )

    parts = (
        widen(vector_sums[0], query_bias.shape[0], mp_rank * head_cols),
        widen(vector_sums[1], value_bias.shape[0], mp_rank * head_cols),
        vector_sums[2],
        widen(vector_sums[3], up_bias.shape[0], mp_rank * unit_cols),
    ) + tuple(vector_sums[4:])
    joined = add_everywhere(
        jnp.concatenate(parts).reshape(-1, 128), mp_count, dp_count
    ).reshape(-1)
    summed, place = [], 0
    for part in parts:
        summed.append(joined[place : place + part.shape[0]])
        place += part.shape[0]
    return (
        jnp.stack(results),
        jnp.stack(input_grads),
        grad_query,
        grad_key,
        grad_value,
        grad_out,
        grad_up,
        grad_down,
    ) + tuple(summed)


def solution(mesh):
    in_specs = (
        P(None, ("dp", "mp"), None),
        P(None, "dp"),
        P("dp", "mp"),
        P("dp", "mp"),
        P("dp", "mp"),
        P("mp", "dp"),
        P("dp", "mp"),
        P("mp", "dp"),
        P(),
        P(),
        P(),
        P(),
        P(),
        P(),
        P(),
        P(),
        P(),
        P(None, ("dp", "mp"), None),
    )
    out_specs = (
        P(None, ("dp", "mp"), None),
        P(None, ("dp", "mp"), None),
        P("dp", "mp"),
        P("dp", "mp"),
        P("dp", "mp"),
        P("mp", "dp"),
        P("dp", "mp"),
        P("mp", "dp"),
        P(),
        P(),
        P(),
        P(),
        P(),
        P(),
        P(),
        P(),
        P(),
    )
    return jax.shard_map(
        functools.partial(on_device, mesh.shape["dp"], mesh.shape["mp"]), mesh=mesh, in_specs=in_specs, out_specs=out_specs, check_vma=False
    )
```

time: 1170 us -> 550 us (0.47)
  waiting for transfers between devices: 666 us -> 180 us
  blocking collectives: 169 us -> 44.9 us
  matrix products: 198 us -> 136 us
  starting transfers between devices: 2.47 us -> 39.2 us
  local copies, waits for them, and re-layouts: 45.8 us -> 59.2 us
    reduce_scatter x9 -> x0, waiting for transfers between devices: 347 us -> none  [the longest x2 82.7 us: on_device(): lax.psum_scatter(matmul(forward_active, forward_down_all), 'mp', scatter_...]
    unnamed x29 -> x4, waiting for transfers between devices: 212 us -> 0.05 us
    ppermute x0 -> x43, waiting for transfers between devices: none -> 180 us  [swap(): return lax.ppermute(block, axis_name, [(i, i ^ bit) for i in range(count)])]
    all_gather x10 -> x2, waiting for transfers between devices: 107 us -> 0.04 us  [the longest x1 0.02 us: on_device(): lax.all_gather(up_weight, 'dp', axis=0, tiled=True)]
    all_gather x4 -> x1, blocking collectives: 129 us -> 44.9 us  [on_device(): lax.all_gather(out_weight.T, 'dp', axis=0, tiled=True)]
    psum x1 -> x0, blocking collectives: 41 us -> none  [on_device(): lax.psum((query_bias_full, value_bias_full, vector_sums[2], up_bias_full,...]
    ppermute x0 -> x43, starting transfers between devices: none -> 39.1 us  [swap(): return lax.ppermute(block, axis_name, [(i, i ^ bit) for i in range(count)])]
    dot_general x12 -> x8, matrix products: 64.7 us -> 33.4 us  [matmul(): return jnp.dot(left_mat, right_mat, preferred_element_type=jnp.float32)]
  transfers between devices with their start and end apart: 24 -> 46, of which waited for: 19 -> 22; matrix products, arithmetic and copies ran while one was open for 22% -> 43% of each run, Pallas kernels for 0% -> 0%
where the time goes in v1:
time: 550 us; the launch traced here: 544 us
  waiting for transfers between devices  180 us (33%)
  matrix products  136 us (25%)
  other arithmetic  66.8 us (12%)
  local copies, waits for them, and re-layouts  59.2 us (11%)
  blocking collectives  44.9 us (8%)
  starting transfers between devices  39.2 us (7%)
  between operations  16.1 us (3%)
    ppermute x43, waiting for transfers between devices, swap(): return lax.ppermute(block, axis_name, [(i, i ^ bit) for i in range(count)])  180 us
    all_gather x1, blocking collectives, on_device(): lax.all_gather(out_weight.T, 'dp', axis=0, tiled=True)  44.9 us
    ppermute x43, starting transfers between devices, swap(): return lax.ppermute(block, axis_name, [(i, i ^ bit) for i in range(count)])  39.1 us
    dot_general x8, matrix products, matmul(): return jnp.dot(left_mat, right_mat, preferred_element_type=jnp.float32)  33.4 us
    unnamed x235, local copies, waits for them, and re-layouts  32.4 us
    dot_general x8, matrix products, inner_rows(): lax.dot_general(left_mat, right_mat, (((0,), (0,)), ((), ())), preferred_...  25.4 us
    dot_general x16, matrix products, outer_cols(): lax.dot_general(left_mat, right_mat, (((1,), (1,)), ((), ())), preferred_...  20.8 us
    dot_general x4, matrix products, one_block(): jnp.einsum('hqd,hkd->hqk', grad_block, value_heads, preferred_element_typ...  12.7 us
  transfers between devices with their start and end apart: 46, of which 22 were waited for; matrix products, arithmetic and copies ran while one was open for 43% of the time, Pallas kernels for 0%

profile of v1, /device:TPU:0, one launch (start us, length us, event | category | flops | bytes accessed | tf_op | source)
XLA Modules:
  0.0 544.1 jit_solution(3210079613150010719)
XLA Ops:
  8.3 4.1 collective-permute-start.2
  12.4 9.0 %collective-permute-done.2 = bf16[1,128,768]{2,1,0:T(8,128)(2,1)S(1)} collective-permute-done((bf16[1,128,768]{2,1,0:T(8,128)(2,1)S(1)}, bf16[1,128,768]{2,1,0:T(8,128)(2,1)S(1)}, u32[]{:S(2)}, u32[]{:S(2)}) %collective-permute-start.2) | collective-permute-done | bytes 196640 | tf_op jit(solution)/shard_map/ppermute | solution.py:164
  25.6 15.0 %collective-permute-done.3 = bf16[2,128,768]{2,1,0:T(8,128)(2,1)S(1)} collective-permute-done((bf16[2,128,768]{2,1,0:T(8,128)(2,1)S(1)}, bf16[2,128,768]{2,1,0:T(8,128)(2,1)S(1)}, u32[]{:S(2)}, u32[]{:S(2)}) %collective-permute-start.3) | collective-permute-done | bytes 393248 | tf_op jit(solution)/shard_map/ppermute | solution.py:164
  43.8 4.6 collective-permute-done.11
  50.5 44.9 %all_gather.9 = bf16[1024,256]{0,1:T(8,128)(2,1)S(1)} all-gather(bf16[128,256]{0,1:T(8,128)(2,1)S(1)} %bitcast.486), channel_id=1, replica_groups=mesh['dp'=8,'mp'=4] {'dp'}, dimensions={0}, use_global_device_ids=true | all-gather | bytes 589824 | tf_op jit(solution)/shard_map/all_gather | solution.py:280
  98.1 3.8 add_convert_fusion.3
  102.5 15.1 %while.55 = (s32[]{:T(128)}, bf16[2,4,512,64]{2,3,1,0:T(8,128)(2,1)S(1)}, f32[2,4,512]{2,1,0:T(4,128)S(1)}, s32[2,512]{1,0:T(2,128)S(1)}, s32[1024]{0:T(1024)S(1...) while((s32[]{:T(128)}, ...), condition=%wide.region_11.12_spmd, body=%wide.region_8.11_spmd.sunk | while | flops 562558976 | bytes 29173876 | solution.py:92
  107.1 3.0 fusion.296
  120.4 3.2 add_convert_fusion.4
  126.2 15.2 %while.54 = (s32[]{:T(128)}, bf16[2,4,512,64]{2,3,1,0:T(8,128)(2,1)S(1)}, f32[2,4,512]{2,1,0:T(4,128)S(1)}, s32[2,512]{1,0:T(2,128)S(1)}, s32[1024]{0:T(1024)S(1...) while((s32[]{:T(128)}, ...), condition=%wide.region_3.4_spmd, body=%wide.region_0.3_spmd.sunk | while | flops 562558976 | bytes 29173876 | solution.py:92
  149.1 11.1 %collective-permute-done.14 = bf16[256,1024]{1,0:T(8,128)(2,1)S(1)} collective-permute-done((bf16[256,1024]{1,0:T(8,128)(2,1)}, bf16[256,1024]{1,0:T(8,128)(2,1)S(1)}, u32[]{:S(2)}, u32[]{:S(2)}) %collective-permute-start.14) | collective-permute-done | bytes 524320 | tf_op jit(solution)/shard_map/ppermute | solution.py:164
  160.9 9.6 %collective-permute-done.6 = bf16[256,1024]{1,0:T(8,128)(2,1)} collective-permute-done((bf16[256,1024]{1,0:T(8,128)(2,1)S(1)}, bf16[256,1024]{1,0:T(8,128)(2,1)}, u32[]{:S(2)}, u32[]{:S(2)}) %collective-permute-start.6) | collective-permute-done | bytes 524320 | tf_op jit(solution)/shard_map/ppermute | solution.py:164
  176.5 12.8 %collective-permute-done.15 = bf16[256,1024]{1,0:T(8,128)(2,1)S(1)} collective-permute-done((bf16[256,1024]{1,0:T(8,128)(2,1)S(1)}, bf16[256,1024]{1,0:T(8,128)(2,1)S(1)}, u32[]{:S(2)}, u32[]{:S(2)}) %collective-permute-start.15) | collective-permute-done | bytes 524320 | tf_op jit(solution)/shard_map/ppermute | solution.py:164
  190.5 8.3 %collective-permute-done.7 = bf16[256,1024]{1,0:T(8,128)(2,1)S(1)} collective-permute-done((bf16[256,1024]{1,0:T(8,128)(2,1)S(1)}, bf16[256,1024]{1,0:T(8,128)(2,1)S(1)}, u32[]{:S(2)}, u32[]{:S(2)}) %collective-permute-start.7) | collective-permute-done | bytes 524320 | tf_op jit(solution)/shard_map/ppermute | solution.py:164
  200.7 4.7 fusion.144
  205.5 9.3 %fusion.78 = (bf16[1024,1024]{1,0:T(8,128)(2,1)}, bf16[1024,1024]{1,0:T(8,128)(2,1)}, bf16[1024,1024]{1,0:T(8,128)(2,1)}, bf16[1024,1024]{1,0:T(8,128)(2,1)}) fusion(f32[1024]{0:T(1024)S(1)} %dynamic-slice-done, f32[1024,1024]{1,0:T(8,128)S(1)} %fusion.144, bf16[1024,1024]{1,0:T(8,128)(2,1)S(1)} %copy-done.109, ...), kind=kOutput, calls=%fused_computation.102 | convolution fusion | flops 2178940928 | bytes 16781312 | tf_op jit(solution)/shard_map/dot_general | solution.py:15
  214.8 3.3 convolution_convert_fusion.6
  225.8 11.3 %collective-permute-done.10 = bf16[256,1024]{1,0:T(8,128)(2,1)S(1)} collective-permute-done((bf16[256,1024]{1,0:T(8,128)(2,1)S(1)}, bf16[256,1024]{1,0:T(8,128)(2,1)S(1)}, u32[]{:S(2)}, u32[]{:S(2)}) %collective-permute-start.10) | collective-permute-done | bytes 524320 | tf_op jit(solution)/shard_map/ppermute | solution.py:164
  237.1 10.7 %collective-permute-done.18 = bf16[256,1024]{1,0:T(8,128)(2,1)S(1)} collective-permute-done((bf16[256,1024]{1,0:T(8,128)(2,1)S(1)}, bf16[256,1024]{1,0:T(8,128)(2,1)S(1)}, u32[]{:S(2)}, u32[]{:S(2)}) %collective-permute-start.18) | collective-permute-done | bytes 524320 | tf_op jit(solution)/shard_map/ppermute | solution.py:164
  255.5 11.9 %collective-permute-done.19 = bf16[256,1024]{1,0:T(8,128)(2,1)S(1)} collective-permute-done((bf16[256,1024]{1,0:T(8,128)(2,1)S(1)}, bf16[256,1024]{1,0:T(8,128)(2,1)S(1)}, u32[]{:S(2)}, u32[]{:S(2)}) %collective-permute-start.19) | collective-permute-done | bytes 524320 | tf_op jit(solution)/shard_map/ppermute | solution.py:164
  277.0 7.1 %collective-permute-done.27 = bf16[256,1024]{1,0:T(8,128)(2,1)} collective-permute-done((bf16[256,1024]{1,0:T(8,128)(2,1)}, bf16[256,1024]{1,0:T(8,128)(2,1)}, u32[]{:S(2)}, u32[]{:S(2)}) %collective-permute-start.27) | collective-permute-done | bytes 524320 | tf_op jit(solution)/shard_map/ppermute | solution.py:164
  286.6 3.8 multiply_convert_fusion.3
  292.5 3.6 multiply_convert_fusion.2
  298.5 3.6 fusion.142
  302.1 3.8 fusion.143
  305.9 3.6 add_convert_fusion.1
  312.7 3.6 add_convert_fusion
  318.4 7.6 %collective-permute-done.22 = bf16[256,1024]{1,0:T(8,128)(2,1)S(1)} collective-permute-done((bf16[256,1024]{1,0:T(8,128)(2,1)S(1)}, bf16[256,1024]{1,0:T(8,128)(2,1)S(1)}, u32[]{:S(2)}, u32[]{:S(2)}) %collective-permute-start.22) | collective-permute-done | bytes 524320 | tf_op jit(solution)/shard_map/ppermute | solution.py:164
  327.1 9.2 %collective-permute-done.30 = bf16[256,1024]{1,0:T(8,128)(2,1)S(1)} collective-permute-done((bf16[256,1024]{1,0:T(8,128)(2,1)S(1)}, bf16[256,1024]{1,0:T(8,128)(2,1)S(1)}, u32[]{:S(2)}, u32[]{:S(2)}) %collective-permute-start.30) | collective-permute-done | bytes 524320 | tf_op jit(solution)/shard_map/ppermute | solution.py:164
  342.9 9.1 %collective-permute-done.23 = bf16[256,1024]{1,0:T(8,128)(2,1)S(1)} collective-permute-done((bf16[256,1024]{1,0:T(8,128)(2,1)S(1)}, bf16[256,1024]{1,0:T(8,128)(2,1)S(1)}, u32[]{:S(2)}, u32[]{:S(2)}) %collective-permute-start.23) | collective-permute-done | bytes 524320 | tf_op jit(solution)/shard_map/ppermute | solution.py:164
  357.8 6.5 %copy.83 = bf16[1024,2048]{1,0:T(8,128)(2,1)} copy(bf16[1024,2048]{0,1:T(8,128)(2,1)} %pad_maximum_fusion) | data formatting | bytes 8388608
  366.4 4.2 collective-permute-done.31
  378.8 25.3 %while.56 = (s32[]{:T(128)}, f32[4,1024,64]{1,2,0:T(8,128)S(1)}, f32[4,1024,64]{1,2,0:T(8,128)}, bf16[2,4,512,64]{2,3,1,0:T(8,128)(2,1)}, s32[2,512]{1,0:T(2,128...) while((s32[]{:T(128)}, f32[4,1024,64]{1,2,0:T(8,128)S(1)}, ...), condition=%wide.region_22.23_spmd.clone, body=%wide.region_20.22_spmd.clone.sunk | while | flops 1375598592 | bytes 87099704 | solution.py:144
  383.7 3.2 multiply_reduce_fusion.14
  396.1 3.2 multiply_reduce_fusion.14
  414.0 24.9 %while.57 = (s32[]{:T(128)}, f32[4,1024,64]{1,2,0:T(8,128)S(1)}, f32[4,1024,64]{1,2,0:T(8,128)}, bf16[2,4,512,64]{2,3,1,0:T(8,128)(2,1)}, s32[2,512]{1,0:T(2,128...) while((s32[]{:T(128)}, f32[4,1024,64]{1,2,0:T(8,128)S(1)}, ...), condition=%wide.region_29.30_spmd.clone, body=%wide.region_27.29_spmd.clone.sunk | while | flops 1375598592 | bytes 85002520 | solution.py:144
  418.5 3.2 multiply_reduce_fusion.15
  430.8 3.2 multiply_reduce_fusion.15
  449.5 3.2 fusion.145
  452.8 3.2 add_convert_fusion.2
  457.5 3.2 reshape_reshape.7
  461.0 4.2 fusion.195
  465.2 4.6 copy.85
  469.8 4.6 copy.86
  476.7 3.6 collective-permute-done.40
  488.3 13.1 %collective-permute-done.42 = f32[96,128]{1,0:T(8,128)S(1)} collective-permute-done((f32[96,128]{1,0:T(8,128)S(1)}, f32[96,128]{1,0:T(8,128)S(1)}, u32[]{:S(2)}, u32[]{:S(2)}) %collective-permute-start.42) | collective-permute-done | bytes 49184 | tf_op jit(solution)/shard_map/ppermute | solution.py:164
  509.6 7.1 %collective-permute-done.36 = bf16[2,128,1024]{2,1,0:T(8,128)(2,1)S(1)} collective-permute-done((bf16[2,128,1024]{2,1,0:T(8,128)(2,1)S(1)}, bf16[2,128,1024]{2,1,0:T(8,128)(2,1)S(1)}, u32[]{:S(2)}, u32[]{:S(2)}) %collective-permute-start.36) | collective-permute-done | bytes 524320 | tf_op jit(solution)/shard_map/ppermute | solution.py:164
  521.5 9.1 %collective-permute-done.34 = bf16[256,1024]{1,0:T(8,128)(2,1)S(1)} collective-permute-done((bf16[256,1024]{1,0:T(8,128)(2,1)S(1)}, bf16[256,1024]{1,0:T(8,128)(2,1)S(1)}, u32[]{:S(2)}, u32[]{:S(2)}) %collective-permute-start.34) | collective-permute-done | bytes 524320 | tf_op jit(solution)/shard_map/ppermute | solution.py:164
  (556 shorter events, 211.6 us)
Async XLA Ops:
  7.2 193.5 %all-gather.3.cloned.1.call-start = ((), (), s32[]{:S(2)}) async-start(), calls=%async_computation.1 | async-start | bytes 2359296 | tf_op jit(solution)/shard_map/all_gather | solution.py:281
  8.3 13.2 %collective-permute-start.2 = (bf16[1,128,768]{2,1,0:T(8,128)(2,1)S(1)}, bf16[1,128,768]{2,1,0:T(8,128)(2,1)S(1)}, u32[]{:S(2)}, u32[]{:S(2)}) collective-permute-start(bf16[1,128,768]{2,1,0:T(8,128)(2,1)S(1)} %maximum_bitcast_fusion.1), channel_id=1, source_target_pairs={{0,16},{4,20},{8,24},{12,28},{16,0},{20,4},{24,8},{28,12},{1,17},{... | collective-permute-start | bytes 589832 | tf_op jit(solution)/shard_map/ppermute | solution.py:164
  12.4 202.4 %all-gather.5.cloned.1.call-start = ((), (), s32[]{:S(2)}) async-start(), calls=%async_computation.2 | async-start | bytes 2359296 | tf_op jit(solution)/shard_map/all_gather | solution.py:282
  22.5 18.1 %collective-permute-start.3 = (bf16[2,128,768]{2,1,0:T(8,128)(2,1)S(1)}, bf16[2,128,768]{2,1,0:T(8,128)(2,1)S(1)}, u32[]{:S(2)}, u32[]{:S(2)}) collective-permute-start(bf16[2,128,768]{2,1,0:T(8,128)(2,1)S(1)} %maximum_bitcast_fusion), channel_id=1, source_target_pairs={{0,8},{4,12},{8,0},{12,4},{16,24},{20,28},{24,16},{28,20},{1,9},{5... | collective-permute-start | bytes 1179656 | tf_op jit(solution)/shard_map/ppermute | solution.py:164
  23.4 74.7 %copy-start.48 = (bf16[256,1024]{1,0:T(8,128)(2,1)}, bf16[256,1024]{1,0:T(8,128)(2,1)S(1)}, u32[]{:S(2)}) copy-start(bf16[256,1024]{1,0:T(8,128)(2,1)S(1)} %get-tuple-element.586) | copy-start | bytes 1572868
  23.4 72.0 %collective-permute-start = (bf16[256,1024]{1,0:T(8,128)(2,1)S(1)}, bf16[256,1024]{1,0:T(8,128)(2,1)}, u32[]{:S(2)}, u32[]{:S(2)}) collective-permute-start(bf16[256,1024]{1,0:T(8,128)(2,1)S(1)} %get-tuple-element.585), channel_id=1, source_target_pairs={{0,2},{1,3},{2,0},{3,1},{4,6},{5,7},{6,4},{7,5},{8,10},{9,11},{10,... | collective-permute-start | bytes 1572872 | tf_op jit(solution)/shard_map/ppermute | solution.py:164
  24.9 23.4 %collective-permute-start.11 = (bf16[256,1024]{1,0:T(8,128)(2,1)S(1)}, bf16[256,1024]{1,0:T(8,128)(2,1)}, u32[]{:S(2)}, u32[]{:S(2)}) collective-permute-start(bf16[256,1024]{1,0:T(8,128)(2,1)S(1)} %get-tuple-element.586), channel_id=1, source_target_pairs={{0,2},{1,3},{2,0},{3,1},{4,6},{5,7},{6,4},{7,5},{8,10},{9,11},{10,... | collective-permute-start | bytes 1572872 | tf_op jit(solution)/shard_map/ppermute | solution.py:164
  40.7 57.0 %collective-permute-start.4 = (bf16[4,128,768]{2,1,0:T(8,128)(2,1)S(1)}, bf16[4,128,768]{2,1,0:T(8,128)(2,1)S(1)}, u32[]{:S(2)}, u32[]{:S(2)}) collective-permute-start(bf16[4,128,768]{2,1,0:T(8,128)(2,1)S(1)} %bitcast.447), channel_id=1, source_target_pairs={{0,4},{4,0},{8,12},{12,8},{16,20},{20,16},{24,28},{28,24},{1,5},{5... | collective-permute-start | bytes 2359304 | tf_op jit(solution)/shard_map/ppermute | solution.py:164
  50.4 47.7 %collective-permute-start.12 = (bf16[512,1024]{1,0:T(8,128)(2,1)}, bf16[512,1024]{1,0:T(8,128)(2,1)}, u32[]{:S(2)}, u32[]{:S(2)}) collective-permute-start(bf16[512,1024]{1,0:T(8,128)(2,1)} %pad_maximum_fusion.16), channel_id=1, source_target_pairs={{0,1},{1,0},{2,3},{3,2},{4,5},{5,4},{6,7},{7,6},{8,9},{9,8},{10,11... | collective-permute-start | bytes 3145736 | tf_op jit(solution)/shard_map/ppermute | solution.py:164
  97.7 22.6 %collective-permute-start.1 = (bf16[512,1024]{1,0:T(8,128)(2,1)}, bf16[512,1024]{1,0:T(8,128)(2,1)}, u32[]{:S(2)}, u32[]{:S(2)}) collective-permute-start(bf16[512,1024]{1,0:T(8,128)(2,1)} %pad_maximum_fusion.14), channel_id=1, source_target_pairs={{0,1},{1,0},{2,3},{3,2},{4,5},{5,4},{6,7},{7,6},{8,9},{9,8},{10,11... | collective-permute-start | bytes 3145736 | tf_op jit(solution)/shard_map/ppermute | solution.py:164
  119.8 22.7 %collective-permute-start.13 = (bf16[512,1024]{1,0:T(8,128)(2,1)}, bf16[512,1024]{1,0:T(8,128)(2,1)}, u32[]{:S(2)}, u32[]{:S(2)}) collective-permute-start(bf16[512,1024]{1,0:T(8,128)(2,1)} %convolution_convert_fusion.5), channel_id=1, source_target_pairs={{0,1},{1,0},{2,3},{3,2},{4,5},{5,4},{6,7},{7,6},{8,9},{9,8},{10,11... | collective-permute-start | bytes 3145736 | tf_op jit(solution)/shard_map/ppermute | solution.py:164
  141.9 4.7 collective-permute-start.5
  145.2 15.0 %collective-permute-start.14 = (bf16[256,1024]{1,0:T(8,128)(2,1)}, bf16[256,1024]{1,0:T(8,128)(2,1)S(1)}, u32[]{:S(2)}, u32[]{:S(2)}) collective-permute-start(bf16[256,1024]{1,0:T(8,128)(2,1)} %slice.531), channel_id=1, source_target_pairs={{0,2},{1,3},{2,0},{3,1},{4,6},{5,7},{6,4},{7,5},{8,10},{9,11},{10,... | collective-permute-start | bytes 1572872 | tf_op jit(solution)/shard_map/ppermute | solution.py:164
  148.4 22.1 %collective-permute-start.6 = (bf16[256,1024]{1,0:T(8,128)(2,1)S(1)}, bf16[256,1024]{1,0:T(8,128)(2,1)}, u32[]{:S(2)}, u32[]{:S(2)}) collective-permute-start(bf16[256,1024]{1,0:T(8,128)(2,1)S(1)} %slice.533), channel_id=1, source_target_pairs={{0,2},{1,3},{2,0},{3,1},{4,6},{5,7},{6,4},{7,5},{8,10},{9,11},{10,... | collective-permute-start | bytes 1572872 | tf_op jit(solution)/shard_map/ppermute | solution.py:164
  149.0 385.1 %reduce-scatter.4.cloned.1.call-start = ((), (), s32[]{:S(2)}) async-start(), calls=%async_computation.3 | async-start | bytes 4718592
  173.2 74.6 %copy-start.5 = (f32[256,1024]{1,0:T(8,128)}, f32[256,1024]{1,0:T(8,128)S(1)}, u32[]{:S(2)}) copy-start(f32[256,1024]{1,0:T(8,128)S(1)} %get-tuple-element.551) | copy-start | bytes 3145732
  174.4 14.9 %collective-permute-start.15 = (bf16[256,1024]{1,0:T(8,128)(2,1)S(1)}, bf16[256,1024]{1,0:T(8,128)(2,1)S(1)}, u32[]{:S(2)}, u32[]{:S(2)}) collective-permute-start(bf16[256,1024]{1,0:T(8,128)(2,1)S(1)} %get-tuple-element.610), channel_id=1, source_target_pairs={{0,2},{1,3},{2,0},{3,1},{4,6},{5,7},{6,4},{7,5},{8,10},{9,11},{10,... | collective-permute-start | bytes 1572872 | tf_op jit(solution)/shard_map/ppermute | solution.py:164
  176.0 22.8 %collective-permute-start.7 = (bf16[256,1024]{1,0:T(8,128)(2,1)S(1)}, bf16[256,1024]{1,0:T(8,128)(2,1)S(1)}, u32[]{:S(2)}, u32[]{:S(2)}) collective-permute-start(bf16[256,1024]{1,0:T(8,128)(2,1)S(1)} %get-tuple-element.609), channel_id=1, source_target_pairs={{0,2},{1,3},{2,0},{3,1},{4,6},{5,7},{6,4},{7,5},{8,10},{9,11},{10,... | collective-permute-start | bytes 1572872 | tf_op jit(solution)/shard_map/ppermute | solution.py:164
  190.5 10.3 %collective-permute-start.16 = (bf16[512,1024]{1,0:T(8,128)(2,1)}, bf16[512,1024]{1,0:T(8,128)(2,1)}, u32[]{:S(2)}, u32[]{:S(2)}) collective-permute-start(bf16[512,1024]{1,0:T(8,128)(2,1)} %pad_maximum_fusion.17), channel_id=1, source_target_pairs={{0,1},{1,0},{2,3},{3,2},{4,5},{5,4},{6,7},{7,6},{8,9},{9,8},{10,11... | collective-permute-start | bytes 3145736 | tf_op jit(solution)/shard_map/ppermute | solution.py:164
  200.6 4.9 collective-permute-start.8
  218.2 2.8 collective-permute-start.9
  219.9 3.9 collective-permute-start.17
  222.3 14.8 %collective-permute-start.10 = (bf16[256,1024]{1,0:T(8,128)(2,1)S(1)}, bf16[256,1024]{1,0:T(8,128)(2,1)S(1)}, u32[]{:S(2)}, u32[]{:S(2)}) collective-permute-start(bf16[256,1024]{1,0:T(8,128)(2,1)S(1)} %slice.532), channel_id=1, source_target_pairs={{0,2},{1,3},{2,0},{3,1},{4,6},{5,7},{6,4},{7,5},{8,10},{9,11},{10,... | collective-permute-start | bytes 1572872 | tf_op jit(solution)/shard_map/ppermute | solution.py:164
  225.2 22.6 %collective-permute-start.18 = (bf16[256,1024]{1,0:T(8,128)(2,1)S(1)}, bf16[256,1024]{1,0:T(8,128)(2,1)S(1)}, u32[]{:S(2)}, u32[]{:S(2)}) collective-permute-start(bf16[256,1024]{1,0:T(8,128)(2,1)S(1)} %slice.530), channel_id=1, source_target_pairs={{0,2},{1,3},{2,0},{3,1},{4,6},{5,7},{6,4},{7,5},{8,10},{9,11},{10,... | collective-permute-start | bytes 1572872 | tf_op jit(solution)/shard_map/ppermute | solution.py:164
  254.0 13.4 %collective-permute-start.19 = (bf16[256,1024]{1,0:T(8,128)(2,1)S(1)}, bf16[256,1024]{1,0:T(8,128)(2,1)S(1)}, u32[]{:S(2)}, u32[]{:S(2)}) collective-permute-start(bf16[256,1024]{1,0:T(8,128)(2,1)S(1)} %convert_element_type.340), channel_id=1, source_target_pairs={{0,2},{1,3},{2,0},{3,1},{4,6},{5,7},{6,4},{7,5},{8,10},{9,11},{10,... | collective-permute-start | bytes 1572872 | tf_op jit(solution)/shard_map/ppermute | solution.py:164
  268.6 18.0 %collective-permute-start.20 = (bf16[512,1024]{1,0:T(8,128)(2,1)}, bf16[512,1024]{1,0:T(8,128)(2,1)}, u32[]{:S(2)}, u32[]{:S(2)}) collective-permute-start(bf16[512,1024]{1,0:T(8,128)(2,1)} %pad_maximum_fusion.19), channel_id=1, source_target_pairs={{0,1},{1,0},{2,3},{3,2},{4,5},{5,4},{6,7},{7,6},{8,9},{9,8},{10,11... | collective-permute-start | bytes 3145736 | tf_op jit(solution)/shard_map/ppermute | solution.py:164
  269.5 14.7 %collective-permute-start.27 = (bf16[256,1024]{1,0:T(8,128)(2,1)}, bf16[256,1024]{1,0:T(8,128)(2,1)}, u32[]{:S(2)}, u32[]{:S(2)}) collective-permute-start(bf16[256,1024]{1,0:T(8,128)(2,1)} %convert_element_type.362), channel_id=1, source_target_pairs={{0,2},{1,3},{2,0},{3,1},{4,6},{5,7},{6,4},{7,5},{8,10},{9,11},{10,... | collective-permute-start | bytes 1572872 | tf_op jit(solution)/shard_map/ppermute | solution.py:164
  285.5 7.0 %collective-permute-start.28 = (bf16[512,1024]{1,0:T(8,128)(2,1)S(1)}, bf16[512,1024]{1,0:T(8,128)(2,1)S(1)}, u32[]{:S(2)}, u32[]{:S(2)}) collective-permute-start(bf16[512,1024]{1,0:T(8,128)(2,1)S(1)} %pad_maximum_fusion.21), channel_id=1, source_target_pairs={{0,1},{1,0},{2,3},{3,2},{4,5},{5,4},{6,7},{7,6},{8,9},{9,8},{10,11... | collective-permute-start | bytes 3145736 | tf_op jit(solution)/shard_map/ppermute | solution.py:164
  291.9 17.6 %collective-permute-start.21 = (bf16[512,1024]{1,0:T(8,128)(2,1)S(1)}, bf16[512,1024]{1,0:T(8,128)(2,1)S(1)}, u32[]{:S(2)}, u32[]{:S(2)}) collective-permute-start(bf16[512,1024]{1,0:T(8,128)(2,1)S(1)} %convolution_convert_fusion.3), channel_id=1, source_target_pairs={{0,1},{1,0},{2,3},{3,2},{4,5},{5,4},{6,7},{7,6},{8,9},{9,8},{10,11... | collective-permute-start | bytes 3145736 | tf_op jit(solution)/shard_map/ppermute | solution.py:164
  297.5 18.9 %collective-permute-start.29 = (bf16[512,1024]{1,0:T(8,128)(2,1)S(1)}, bf16[512,1024]{1,0:T(8,128)(2,1)S(1)}, u32[]{:S(2)}, u32[]{:S(2)}) collective-permute-start(bf16[512,1024]{1,0:T(8,128)(2,1)S(1)} %convolution_convert_fusion.2), channel_id=1, source_target_pairs={{0,1},{1,0},{2,3},{3,2},{4,5},{5,4},{6,7},{7,6},{8,9},{9,8},{10,11... | collective-permute-start | bytes 3145736 | tf_op jit(solution)/shard_map/ppermute | solution.py:164
  311.2 14.9 %collective-permute-start.22 = (bf16[256,1024]{1,0:T(8,128)(2,1)S(1)}, bf16[256,1024]{1,0:T(8,128)(2,1)S(1)}, u32[]{:S(2)}, u32[]{:S(2)}) collective-permute-start(bf16[256,1024]{1,0:T(8,128)(2,1)S(1)} %slice.529), channel_id=1, source_target_pairs={{0,2},{1,3},{2,0},{3,1},{4,6},{5,7},{6,4},{7,5},{8,10},{9,11},{10,... | collective-permute-start | bytes 1572872 | tf_op jit(solution)/shard_map/ppermute | solution.py:164
  317.7 18.6 %collective-permute-start.30 = (bf16[256,1024]{1,0:T(8,128)(2,1)S(1)}, bf16[256,1024]{1,0:T(8,128)(2,1)S(1)}, u32[]{:S(2)}, u32[]{:S(2)}) collective-permute-start(bf16[256,1024]{1,0:T(8,128)(2,1)S(1)} %slice.527), channel_id=1, source_target_pairs={{0,2},{1,3},{2,0},{3,1},{4,6},{5,7},{6,4},{7,5},{8,10},{9,11},{10,... | collective-permute-start | bytes 1572872 | tf_op jit(solution)/shard_map/ppermute | solution.py:164
  338.9 13.1 %collective-permute-start.23 = (bf16[256,1024]{1,0:T(8,128)(2,1)S(1)}, bf16[256,1024]{1,0:T(8,128)(2,1)S(1)}, u32[]{:S(2)}, u32[]{:S(2)}) collective-permute-start(bf16[256,1024]{1,0:T(8,128)(2,1)S(1)} %convert_element_type.346), channel_id=1, source_target_pairs={{0,2},{1,3},{2,0},{3,1},{4,6},{5,7},{6,4},{7,5},{8,10},{9,11},{10,... | collective-permute-start | bytes 1572872 | tf_op jit(solution)/shard_map/ppermute | solution.py:164
  353.1 19.8 %collective-permute-start.24 = (bf16[512,1024]{1,0:T(8,128)(2,1)}, bf16[512,1024]{1,0:T(8,128)(2,1)}, u32[]{:S(2)}, u32[]{:S(2)}) collective-permute-start(bf16[512,1024]{1,0:T(8,128)(2,1)} %pad_maximum_fusion.20), channel_id=1, source_target_pairs={{0,1},{1,0},{2,3},{3,2},{4,5},{5,4},{6,7},{7,6},{8,9},{9,8},{10,11... | collective-permute-start | bytes 3145736 | tf_op jit(solution)/shard_map/ppermute | solution.py:164
  355.9 14.7 %collective-permute-start.31 = (bf16[256,1024]{1,0:T(8,128)(2,1)}, bf16[256,1024]{1,0:T(8,128)(2,1)}, u32[]{:S(2)}, u32[]{:S(2)}) collective-permute-start(bf16[256,1024]{1,0:T(8,128)(2,1)} %convert_element_type.368), channel_id=1, source_target_pairs={{0,2},{1,3},{2,0},{3,1},{4,6},{5,7},{6,4},{7,5},{8,10},{9,11},{10,... | collective-permute-start | bytes 1572872 | tf_op jit(solution)/shard_map/ppermute | solution.py:164
  372.9 35.6 %collective-permute-start.32 = (bf16[512,1024]{1,0:T(8,128)(2,1)}, bf16[512,1024]{1,0:T(8,128)(2,1)}, u32[]{:S(2)}, u32[]{:S(2)}) collective-permute-start(bf16[512,1024]{1,0:T(8,128)(2,1)} %pad_maximum_fusion.22), channel_id=1, source_target_pairs={{0,1},{1,0},{2,3},{3,2},{4,5},{5,4},{6,7},{7,6},{8,9},{9,8},{10,11... | collective-permute-start | bytes 3145736 | tf_op jit(solution)/shard_map/ppermute | solution.py:164
  443.5 17.2 %collective-permute-start.38 = (f32[96,128]{1,0:T(8,128)S(1)}, f32[96,128]{1,0:T(8,128)S(1)}, u32[]{:S(2)}, u32[]{:S(2)}) collective-permute-start(f32[96,128]{1,0:T(8,128)S(1)} %bitcast.481), channel_id=1, source_target_pairs={{0,2},{1,3},{2,0},{3,1},{4,6},{5,7},{6,4},{7,5},{8,10},{9,11},{10,... | collective-permute-start | bytes 147464 | tf_op jit(solution)/shard_map/ppermute | solution.py:164
  460.7 13.6 %collective-permute-start.39 = (f32[96,128]{1,0:T(8,128)S(1)}, f32[96,128]{1,0:T(8,128)S(1)}, u32[]{:S(2)}, u32[]{:S(2)}) collective-permute-start(f32[96,128]{1,0:T(8,128)S(1)} %bitcast_add_fusion.1), channel_id=1, source_target_pairs={{0,1},{1,0},{2,3},{3,2},{4,5},{5,4},{6,7},{7,6},{8,9},{9,8},{10,11... | collective-permute-start | bytes 147464 | tf_op jit(solution)/shard_map/ppermute | solution.py:164
  474.4 5.8 %collective-permute-start.40 = (f32[96,128]{1,0:T(8,128)S(1)}, f32[96,128]{1,0:T(8,128)S(1)}, u32[]{:S(2)}, u32[]{:S(2)}) collective-permute-start(f32[96,128]{1,0:T(8,128)S(1)} %fusion.250), channel_id=1, source_target_pairs={{0,16},{4,20},{8,24},{12,28},{16,0},{20,4},{24,8},{28,12},{1,17},{... | collective-permute-start | bytes 147464 | tf_op jit(solution)/shard_map/ppermute | solution.py:164
  475.0 27.7 %collective-permute-start.35 = (bf16[4,128,1024]{2,1,0:T(8,128)(2,1)S(1)}, bf16[4,128,1024]{2,1,0:T(8,128)(2,1)S(1)}, u32[]{:S(2)}, u32[]{:S(2)}) collective-permute-start(bf16[4,128,1024]{2,1,0:T(8,128)(2,1)S(1)} %select_bitcast_fusion), channel_id=1, source_target_pairs={{0,4},{4,0},{8,12},{12,8},{16,20},{20,16},{24,28},{28,24},{1,5},{5... | collective-permute-start | bytes 3145736 | tf_op jit(solution)/shard_map/ppermute | solution.py:164
  480.2 4.2 collective-permute-start.41
  484.4 17.0 %collective-permute-start.42 = (f32[96,128]{1,0:T(8,128)S(1)}, f32[96,128]{1,0:T(8,128)S(1)}, u32[]{:S(2)}, u32[]{:S(2)}) collective-permute-start(f32[96,128]{1,0:T(8,128)S(1)} %add.421), channel_id=1, source_target_pairs={{0,4},{4,0},{8,12},{12,8},{16,20},{20,16},{24,28},{28,24},{1,5},{5... | collective-permute-start | bytes 147464 | tf_op jit(solution)/shard_map/ppermute | solution.py:164
  487.7 17.5 %collective-permute-start.25 = (bf16[512,1024]{1,0:T(8,128)(2,1)S(1)}, bf16[512,1024]{1,0:T(8,128)(2,1)S(1)}, u32[]{:S(2)}, u32[]{:S(2)}) collective-permute-start(bf16[512,1024]{1,0:T(8,128)(2,1)S(1)} %convolution_convert_fusion.1), channel_id=1, source_target_pairs={{0,1},{1,0},{2,3},{3,2},{4,5},{5,4},{6,7},{7,6},{8,9},{9,8},{10,11... | collective-permute-start | bytes 3145736 | tf_op jit(solution)/shard_map/ppermute | solution.py:164
  487.8 19.4 %collective-permute-start.33 = (bf16[512,1024]{1,0:T(8,128)(2,1)S(1)}, bf16[512,1024]{1,0:T(8,128)(2,1)S(1)}, u32[]{:S(2)}, u32[]{:S(2)}) collective-permute-start(bf16[512,1024]{1,0:T(8,128)(2,1)S(1)} %convolution_convert_fusion), channel_id=1, source_target_pairs={{0,1},{1,0},{2,3},{3,2},{4,5},{5,4},{6,7},{7,6},{8,9},{9,8},{10,11... | collective-permute-start | bytes 3145736 | tf_op jit(solution)/shard_map/ppermute | solution.py:164
  503.3 13.4 %collective-permute-start.36 = (bf16[2,128,1024]{2,1,0:T(8,128)(2,1)S(1)}, bf16[2,128,1024]{2,1,0:T(8,128)(2,1)S(1)}, u32[]{:S(2)}, u32[]{:S(2)}) collective-permute-start(bf16[2,128,1024]{2,1,0:T(8,128)(2,1)S(1)} %fusion.160), channel_id=1, source_target_pairs={{0,8},{4,12},{8,0},{12,4},{16,24},{20,28},{24,16},{28,20},{1,9},{5... | collective-permute-start | bytes 1572872 | tf_op jit(solution)/shard_map/ppermute | solution.py:164
  506.3 14.9 %collective-permute-start.26 = (bf16[256,1024]{1,0:T(8,128)(2,1)S(1)}, bf16[256,1024]{1,0:T(8,128)(2,1)S(1)}, u32[]{:S(2)}, u32[]{:S(2)}) collective-permute-start(bf16[256,1024]{1,0:T(8,128)(2,1)S(1)} %slice.528), channel_id=1, source_target_pairs={{0,2},{1,3},{2,0},{3,1},{4,6},{5,7},{6,4},{7,5},{8,10},{9,11},{10,... | collective-permute-start | bytes 1572872 | tf_op jit(solution)/shard_map/ppermute | solution.py:164
  508.3 22.3 %collective-permute-start.34 = (bf16[256,1024]{1,0:T(8,128)(2,1)S(1)}, bf16[256,1024]{1,0:T(8,128)(2,1)S(1)}, u32[]{:S(2)}, u32[]{:S(2)}) collective-permute-start(bf16[256,1024]{1,0:T(8,128)(2,1)S(1)} %slice.526), channel_id=1, source_target_pairs={{0,2},{1,3},{2,0},{3,1},{4,6},{5,7},{6,4},{7,5},{8,10},{9,11},{10,... | collective-permute-start | bytes 1572872 | tf_op jit(solution)/shard_map/ppermute | solution.py:164
  517.1 15.4 %collective-permute-start.37 = (bf16[1,128,1024]{2,1,0:T(8,128)(2,1)S(1)}, bf16[1,128,1024]{2,1,0:T(8,128)(2,1)S(1)}, u32[]{:S(2)}, u32[]{:S(2)}) collective-permute-start(bf16[1,128,1024]{2,1,0:T(8,128)(2,1)S(1)} %fusion.162), channel_id=1, source_target_pairs={{0,16},{4,20},{8,24},{12,28},{16,0},{20,4},{24,8},{28,12},{1,17},{... | collective-permute-start | bytes 786440 | tf_op jit(solution)/shard_map/ppermute | solution.py:164
  (127 other events, 785.5 us)
Sparse Core Ops, SparseCore 0:
  12.5 68.0 all-gather.2
  149.1 50.4 all-gather.4
  364.4 86.8 reduce-scatter.3

commit v2 on v1

--- a/solution.py
+++ b/solution.py
@@ -3,6 +3,8 @@
 import jax
 import jax.numpy as jnp
 from jax import lax
+from jax.experimental import pallas as pl
+from jax.experimental.pallas import tpu as pltpu
 from jax.sharding import PartitionSpec as P
 
 HDIM = 64
@@ -50,106 +52,129 @@
     return jax.nn.gelu(values_in, approximate=False)
 
 
-def head_major(matrix, head_count):
-    return matrix.reshape(matrix.shape[0], head_count, HDIM).transpose(1, 0, 2)
-
-
-def head_blocks(matrix, head_count, block_rows):
-    row_count = matrix.shape[0]
-    return (
-        head_major(matrix, head_count)
-        .reshape(head_count, row_count // block_rows, block_rows, HDIM)
-        .transpose(1, 0, 2, 3)
-    )
-
-
-def score_block(query_block, key_heads, query_segs, key_segs):
-    raw_scores = jnp.einsum(
-        "hqd,hkd->hqk", query_block, key_heads, preferred_element_type=jnp.float32
-    )
-    same_doc = (query_segs[:, None] == key_segs[None, :])[None]
-    return jnp.where(same_doc, raw_scores * HDIM ** (-0.5), -1000000000.0)
-
-
-def attention_forward(queries, key_rows, value_rows, seg_row, head_count):
-    row_count = queries.shape[0]
-    block_rows = min(512, row_count)
-    key_heads = head_major(key_rows, head_count)
-    value_heads = head_major(value_rows, head_count)
-
-    def one_block(pieces):
-        query_block, query_segs = pieces
-        scores = score_block(query_block, key_heads, query_segs, seg_row)
-        top_val = jnp.max(scores, axis=-1, keepdims=True)
-        exponent = jnp.exp(scores - top_val)
-        totals = jnp.sum(exponent, axis=-1, keepdims=True)
-        probabilities = (exponent / totals).astype(jnp.bfloat16)
-        context = jnp.einsum(
-            "hqk,hkd->hqd", probabilities, value_heads, preferred_element_type=jnp.float32
-        )
-        return (context, (top_val + jnp.log(totals))[..., 0])
-
-    context, log_totals = lax.map(
-        one_block, (head_blocks(queries, head_count, block_rows), seg_row.reshape(-1, block_rows))
-    )
-    return (context.transpose(0, 2, 1, 3).reshape(row_count, head_count * HDIM), log_totals)
-
-
-def attention_backward(
-    queries, key_rows, value_rows, seg_row, log_totals, grad_context, head_count
+def head_lanes(matrix, index):
+    lane = lax.broadcasted_iota(jnp.int32, matrix.shape, 1)
+    return jnp.where(lane // HDIM == index, matrix, jnp.zeros_like(matrix))
+
+
+def forward_kernel(query_ref, key_ref, value_ref, column_ref, row_ref, context_ref, lse_ref):
+    rows, width = query_ref.shape
+    block = min(256, rows)
+    key_rows = key_ref[...]
+    values = [head_lanes(value_ref[...], index) for index in range(width // HDIM)]
+    key_segs = row_ref[...]
+
+    def one_block(step, carry):
+        span = pl.ds(pl.multiple_of(step * block, block), block)
+        queries = query_ref[span, :] * jnp.asarray(HDIM ** (-0.5), jnp.bfloat16)
+        same_doc = column_ref[span, :] == key_segs
+        context = jnp.zeros((block, width), jnp.float32)
+        for index in range(width // HDIM):
+            scores = outer_cols(head_lanes(queries, index), key_rows)
+            scores = jnp.where(same_doc, scores, -1000000000.0)
+            top_val = jnp.max(scores, axis=-1, keepdims=True)
+            exponent = jnp.exp(scores - top_val)
+            total = jnp.sum(exponent, axis=-1, keepdims=True)
+            context += matmul(exponent.astype(jnp.bfloat16), values[index]) / total
+            lse_ref[0, span, index : index + 1] = top_val + jnp.log(total)
+        context_ref[span, :] = context.astype(jnp.bfloat16)
+        return carry
+
+    lax.fori_loop(0, rows // block, one_block, 0)
+
+
+def attention_forward(queries, key_rows, value_rows, seg_row):
+    rows, head_cols = queries.shape
+    width = min(128, head_cols)
+    pairs = head_cols // width
+    columns = pl.BlockSpec((rows, width), lambda pair: (0, pair))
+    work = rows * rows * (head_cols // HDIM)
+    return pl.pallas_call(
+        forward_kernel,
+        grid=(pairs,),
+        in_specs=[
+            columns,
+            columns,
+            columns,
+            pl.BlockSpec((rows, 1), lambda pair: (0, 0)),
+            pl.BlockSpec((1, rows), lambda pair: (0, 0)),
+        ],
+        out_specs=[columns, pl.BlockSpec((1, rows, width // HDIM), lambda pair: (pair, 0, 0))],
+        out_shape=[
+            jax.ShapeDtypeStruct((rows, head_cols), jnp.bfloat16),
+            jax.ShapeDtypeStruct((pairs, rows, width // HDIM), jnp.float32),
+        ],
+        compiler_params=pltpu.CompilerParams(vmem_limit_bytes=32 * 1024 * 1024),
+        cost_estimate=pl.CostEstimate(
+            flops=4 * HDIM * work, bytes_accessed=8 * rows * head_cols, transcendentals=work
+        ),
+    )(queries, key_rows, value_rows, seg_row[:, None], seg_row[None, :])
+
+
+def backward_kernel(
+    query_ref, key_ref, value_ref, grad_ref, column_ref, row_ref, lse_ref,
+    query_grad_ref, key_grad_ref, value_grad_ref, key_sum, value_sum,
 ):
-    row_count = queries.shape[0]
-    block_rows = min(512, row_count)
-    key_heads = head_major(key_rows, head_count)
-    value_heads = head_major(value_rows, head_count)
-    scale_val = HDIM ** (-0.5)
-
-    def one_block(sum_pair, pieces):
-        query_block, grad_block, query_segs, block_lse = pieces
-        scores = score_block(query_block, key_heads, query_segs, seg_row)
-        probabilities = jnp.exp(scores - block_lse[..., None])
-        grad_probs = jnp.einsum(
-            "hqd,hkd->hqk", grad_block, value_heads, preferred_element_type=jnp.float32
-        )
-        grad_scores = (
-            probabilities
-            * (grad_probs - jnp.sum(grad_probs * probabilities, axis=-1, keepdims=True))
-        ).astype(jnp.bfloat16)
-        grad_query = (
-            jnp.einsum("hqk,hkd->hqd", grad_scores, key_heads, preferred_element_type=jnp.float32)
-            * scale_val
-        )
-        key_sum = (
-            sum_pair[0]
-            + jnp.einsum(
-                "hqk,hqd->hkd", grad_scores, query_block, preferred_element_type=jnp.float32
-            )
-            * scale_val
-        )
-        value_sum = sum_pair[1] + jnp.einsum(
-            "hqk,hqd->hkd",
-            probabilities.astype(jnp.bfloat16),
-            grad_block,
-            preferred_element_type=jnp.float32,
-        )
-        return ((key_sum, value_sum), grad_query)
-
-    zero_acc = jnp.zeros((head_count, row_count, HDIM), jnp.float32)
-    pieces = (
-        head_blocks(queries, head_count, block_rows),
-        head_blocks(grad_context, head_count, block_rows),
-        seg_row.reshape(-1, block_rows),
-        log_totals,
-    )
-    (key_sum, value_sum), grad_query = lax.scan(one_block, (zero_acc, zero_acc), pieces)
-    grad_query = grad_query.transpose(0, 2, 1, 3).reshape(row_count, head_count * HDIM)
-    key_sum = key_sum.transpose(1, 0, 2).reshape(row_count, head_count * HDIM)
-    value_sum = value_sum.transpose(1, 0, 2).reshape(row_count, head_count * HDIM)
-    return (
-        grad_query.astype(jnp.bfloat16),
-        key_sum.astype(jnp.bfloat16),
-        value_sum.astype(jnp.bfloat16),
-    )
+    rows, width = query_ref.shape
+    block = min(256, rows)
+    key_rows, value_rows = key_ref[...], value_ref[...]
+    keys = [head_lanes(key_rows, index) for index in range(width // HDIM)]
+    key_segs = row_ref[...]
+    key_sum[...] = jnp.zeros_like(key_sum)
+    value_sum[...] = jnp.zeros_like(value_sum)
+
+    def one_block(step, carry):
+        span = pl.ds(pl.multiple_of(step * block, block), block)
+        queries = query_ref[span, :] * jnp.asarray(HDIM ** (-0.5), jnp.bfloat16)
+        grads = grad_ref[span, :]
+        same_doc = column_ref[span, :] == key_segs
+        query_grad = jnp.zeros((block, width), jnp.float32)
+        for index in range(width // HDIM):
+            query_head = head_lanes(queries, index)
+            grad_head = head_lanes(grads, index)
+            scores = outer_cols(query_head, key_rows)
+            scores = jnp.where(same_doc, scores, -1000000000.0)
+            probs = jnp.exp(scores - lse_ref[0, span, index : index + 1])
+            grad_probs = outer_cols(grad_head, value_rows)
+            slope = jnp.sum(grad_probs * probs, axis=-1, keepdims=True)
+            grad_scores = (probs * (grad_probs - slope)).astype(jnp.bfloat16)
+            query_grad += matmul(grad_scores, keys[index])
+            key_sum[...] += inner_rows(grad_scores, query_head)
+            value_sum[...] += inner_rows(probs.astype(jnp.bfloat16), grad_head)
+        query_grad_ref[span, :] = (query_grad * HDIM ** (-0.5)).astype(jnp.bfloat16)
+        return carry
+
+    lax.fori_loop(0, rows // block, one_block, 0)
+    key_grad_ref[...] = key_sum[...].astype(jnp.bfloat16)
+    value_grad_ref[...] = value_sum[...].astype(jnp.bfloat16)
+
+
+def attention_backward(queries, key_rows, value_rows, seg_row, lse, grad_context):
+    rows, head_cols = queries.shape
+    width = min(128, head_cols)
+    pairs = head_cols // width
+    columns = pl.BlockSpec((rows, width), lambda pair: (0, pair))
+    work = rows * rows * (head_cols // HDIM)
+    return pl.pallas_call(
+        backward_kernel,
+        grid=(pairs,),
+        in_specs=[
+            columns,
+            columns,
+            columns,
+            columns,
+            pl.BlockSpec((rows, 1), lambda pair: (0, 0)),
+            pl.BlockSpec((1, rows), lambda pair: (0, 0)),
+            pl.BlockSpec((1, rows, width // HDIM), lambda pair: (pair, 0, 0)),
+        ],
+        out_specs=[columns] * 3,
+        out_shape=[jax.ShapeDtypeStruct((rows, head_cols), jnp.bfloat16)] * 3,
+        scratch_shapes=[pltpu.VMEM((rows, width), jnp.float32)] * 2,
+        compiler_params=pltpu.CompilerParams(vmem_limit_bytes=32 * 1024 * 1024),
+        cost_estimate=pl.CostEstimate(
+            flops=10 * HDIM * work, bytes_accessed=14 * rows * head_cols, transcendentals=work
+        ),
+    )(queries, key_rows, value_rows, grad_context, seg_row[:, None], seg_row[None, :], lse)
 
 
 def steps_of(count):
@@ -191,7 +216,11 @@
             kept = kept[:half]
         kept = kept + came.astype(jnp.float32)
         half //= 2
-    return kept
+    return kept, sent
+
+
+def after(value, earlier):
+    return value if earlier is None else lax.optimization_barrier((value, earlier))[0]
 
 
 def gather_shards(block, count):
@@ -263,7 +292,6 @@
     micro_count = inputs.shape[0]
     head_cols = query_weight.shape[1]
     unit_cols = up_weight.shape[1]
-    head_count = head_cols // HDIM
     mp_rank = lax.axis_index("mp")
     own_rows = inputs.shape[1]
     rows = own_rows * mp_count
@@ -276,14 +304,15 @@
     qkv_all = gather_shards(
         jnp.concatenate([query_weight, key_weight, value_weight], axis=1), dp_count
     )
-    out_t, up_all, down_t = (
-        lax.all_gather(out_weight.T, "dp", axis=0, tiled=True),
+    out_t = gather_shards(out_weight.T, dp_count)
+    up_all, down_t = (
         lax.all_gather(up_weight, "dp", axis=0, tiled=True),
         lax.all_gather(down_weight.T, "dp", axis=0, tiled=True),
     )
 
     results = []
     saved_list = []
+    heads_sent = units_sent = None
     for micro in range(micro_count):
         own_tokens = inputs[micro]
         seg_blocks = segments[micro].reshape(mp_count, own_rows)
@@ -292,22 +321,23 @@
         )
         token_rows = gather_rows(own_tokens, mp_count)
         qkv = (matmul(token_rows, qkv_all) + qkv_bias).astype(jnp.bfloat16)
+        qkv = after(qkv, heads_sent)
         queries = qkv[:, :head_cols]
         key_rows = qkv[:, head_cols : 2 * head_cols]
         value_rows = qkv[:, 2 * head_cols :]
-        context, log_totals = attention_forward(queries, key_rows, value_rows, seg_row, head_count)
-        context = context.astype(jnp.bfloat16)
-        attention_out = scatter_rows(
+        context, log_totals = attention_forward(queries, key_rows, value_rows, seg_row)
+        attention_out, heads_sent = scatter_rows(
             lambda low, high: outer_cols(context[low:high], out_t), rows, mp_count
         )
         first_out, first_normed, first_inverse = norm_forward(
             own_tokens.astype(jnp.float32) + attention_out + out_bias, first_gain, first_shift
         )
         first_rows = gather_rows(first_out.astype(jnp.bfloat16), mp_count)
+        first_rows = after(first_rows, units_sent)
         active, slope = lax.optimization_barrier(
             gelu_pair(matmul(first_rows, up_all) + up_bias_own)
         )
-        feed_out = scatter_rows(
+        feed_out, units_sent = scatter_rows(
             lambda low, high: outer_cols(active[low:high], down_t), rows, mp_count
         )
         final_out, second_normed, second_inverse = norm_forward(
@@ -324,6 +354,7 @@
     vector_sums = None
     input_grads = []
     pieces = []
+    heads_sent = units_sent = None
     for micro in range(micro_count):
         (
             token_rows, seg_row, queries, key_rows, value_rows, log_totals, context,
@@ -335,22 +366,25 @@
             incoming, second_normed, second_inverse, second_gain
         )
         feed_rows = gather_rows(grad_second.astype(jnp.bfloat16), mp_count)
+        feed_rows = after(feed_rows, units_sent)
         grad_hidden = lax.optimization_barrier(
             (matmul(feed_rows, down_t) * slope.astype(jnp.float32)).astype(jnp.bfloat16)
         )
-        grad_first = grad_second + scatter_rows(
+        unit_terms, units_sent = scatter_rows(
             lambda low, high: outer_cols(grad_hidden[low:high], up_all), rows, mp_count
         )
+        grad_first = grad_second + unit_terms
         grad_resid, grad_first_gain, grad_first_shift = norm_backward(
             grad_first, first_normed, first_inverse, first_gain
         )
         attention_rows = gather_rows(grad_resid.astype(jnp.bfloat16), mp_count)
+        attention_rows = after(attention_rows, heads_sent)
         grad_context = matmul(attention_rows, out_t).astype(jnp.bfloat16)
         grad_queries, grad_keys, grad_values = attention_backward(
-            queries, key_rows, value_rows, seg_row, log_totals, grad_context, head_count
+            queries, key_rows, value_rows, seg_row, log_totals, grad_context
         )
         grad_qkv = jnp.concatenate([grad_queries, grad_keys, grad_values], axis=1)
-        token_grad = scatter_rows(
+        token_grad, heads_sent = scatter_rows(
             lambda low, high: outer_cols(grad_qkv[low:high], qkv_all), rows, mp_count
         )
         input_grads.append(grad_resid + token_grad)

time: 550 us -> 491 us (0.89)
  matrix products: 136 us -> 70.8 us
  Pallas kernels: 0 us -> 58.1 us
  blocking collectives: 44.9 us -> 0 us
  waiting for transfers between devices: 180 us -> 208 us
  other arithmetic: 66.8 us -> 39.7 us
  local copies, waits for them, and re-layouts: 59.2 us -> 49.4 us
    pallas_call x0 -> x4, Pallas kernels: none -> 58.1 us  [the longest x2 36.4 us: attention_backward(): pl.pallas_call(backward_kernel, grid=(pairs,), in_specs=[columns, columns...]
    dot_general x28 -> x0, matrix products: 56.7 us -> none  [the longest x4 12.7 us: one_block(): jnp.einsum('hqd,hkd->hqk', grad_block, value_heads, preferred_element_typ...]
    all_gather x1 -> x0, blocking collectives: 44.9 us -> none  [on_device(): lax.all_gather(out_weight.T, 'dp', axis=0, tiled=True)]
    ppermute x43 -> x46, waiting for transfers between devices: 180 us -> 195 us  [swap(): return lax.ppermute(block, axis_name, [(i, i ^ bit) for i in range(count)])]
    all_gather x1, waiting for transfers between devices: 0.02 us -> 13.4 us  [on_device(): lax.all_gather(down_weight.T, 'dp', axis=0, tiled=True)]
    convert_element_type x8 -> x0, other arithmetic: 11.4 us -> none  [the longest x4 9.51 us: one_block(): grad_scores = (probabilities * (grad_probs - jnp.sum(grad_probs * probabi...]
    reduce_sum x4 -> x0, other arithmetic: 9.33 us -> none  [one_block(): totals = jnp.sum(exponent, axis=-1, keepdims=True)]
    dot_general x8, matrix products: 33.4 us -> 25.4 us  [matmul(): return jnp.dot(left_mat, right_mat, preferred_element_type=jnp.float32)]
  transfers between devices with their start and end apart: 46 -> 49, of which waited for: 22 -> 26; matrix products, arithmetic and copies ran while one was open for 43% -> 27% of each run, Pallas kernels for 0% -> 12%
where the time goes in v2:
time: 491 us; the launch traced here: 482 us
  waiting for transfers between devices  208 us (42%)
  matrix products  70.8 us (14%)
  Pallas kernels  58.1 us (12%)
  local copies, waits for them, and re-layouts  49.4 us (10%)
  other arithmetic  39.7 us (8%)
  starting transfers between devices  39.6 us (8%)
  between operations  15.8 us (3%)
    ppermute x46, waiting for transfers between devices, swap(): return lax.ppermute(block, axis_name, [(i, i ^ bit) for i in range(count)])  195 us
    ppermute x46, starting transfers between devices, swap(): return lax.ppermute(block, axis_name, [(i, i ^ bit) for i in range(count)])  38.9 us
    pallas_call x2, Pallas kernels, attention_backward(): pl.pallas_call(backward_kernel, grid=(pairs,), in_specs=[columns, columns...  36.4 us
    unnamed x164, local copies, waits for them, and re-layouts  31.3 us
    dot_general x8, matrix products, matmul(): return jnp.dot(left_mat, right_mat, preferred_element_type=jnp.float32)  25.4 us
    dot_general x8, matrix products, inner_rows(): lax.dot_general(left_mat, right_mat, (((0,), (0,)), ((), ())), preferred_...  22.7 us
    dot_general x16, matrix products, outer_cols(): lax.dot_general(left_mat, right_mat, (((1,), (1,)), ((), ())), preferred_...  22.7 us
    pallas_call x2, Pallas kernels, attention_forward(): pl.pallas_call(forward_kernel, grid=(pairs,), in_specs=[columns, columns,...  21.7 us
  transfers between devices with their start and end apart: 49, of which 26 were waited for; matrix products, arithmetic and copies ran while one was open for 27% of the time, Pallas kernels for 12%

profile of v2, /device:TPU:0, one launch (start us, length us, event | category | flops | bytes accessed | tf_op | source)
XLA Modules:
  0.0 481.8 jit_solution(1389415036389753031)
XLA Ops:
  8.3 4.1 collective-permute-start.5
  16.9 4.3 collective-permute-start.6
  21.2 3.7 collective-permute-done.2
  25.2 2.5 collective-permute-done.6
  29.4 6.5 %collective-permute-done.3 = bf16[2,128,768]{2,1,0:T(8,128)(2,1)S(1)} collective-permute-done((bf16[2,128,768]{2,1,0:T(8,128)(2,1)S(1)}, bf16[2,128,768]{2,1,0:T(8,128)(2,1)S(1)}, u32[]{:S(2)}, u32[]{:S(2)}) %collective-permute-start.3) | collective-permute-done | bytes 393248 | tf_op jit(solution)/shard_map/ppermute | solution.py:189
  44.5 10.1 %collective-permute-done.4 = bf16[4,128,768]{2,1,0:T(8,128)(2,1)} collective-permute-done((bf16[4,128,768]{2,1,0:T(8,128)(2,1)S(1)}, bf16[4,128,768]{2,1,0:T(8,128)(2,1)}, u32[]{:S(2)}, u32[]{:S(2)}) %collective-permute-start.4) | collective-permute-done | bytes 786464 | tf_op jit(solution)/shard_map/ppermute | solution.py:189
  56.1 3.2 add_convert_fusion.4
  59.5 10.8 %shard_map.305 = (bf16[1024,256]{1,0:T(8,128)(2,1)S(1)}, f32[2,1024,2]{2,1,0:T(8,128)S(1)}) custom-call(bf16[1024,256]{1,0:T(8,128)(2,1)S(1)} %get-tuple-element.153.query_ref, bf16[1024,256]{1,0:T(8,128)(2,1)S(1)} %get-tuple-element.152.key_ref, bf16[1024,256]{1,0:T(8,128)(2,1)S(1)} %get-tuple-element.151.value_ref, s32[1024,1]{1,0:T(8,128)S(1)} %copy.62.column_ref, ...), custom_call_target="tpu_custom_call" | custom-call | flops 1073741824 | bytes 2097152 | tf_op jit(solution)/shard_map/pallas_call | solution.py:92
  72.2 3.8 add_convert_fusion.3
  80.1 10.9 %shard_map.306 = (bf16[1024,256]{1,0:T(8,128)(2,1)S(1)}, f32[2,1024,2]{2,1,0:T(8,128)S(1)}) custom-call(bf16[1024,256]{1,0:T(8,128)(2,1)S(1)} %get-tuple-element.150.query_ref, bf16[1024,256]{1,0:T(8,128)(2,1)S(1)} %get-tuple-element.149.key_ref, bf16[1024,256]{1,0:T(8,128)(2,1)S(1)} %get-tuple-element.148.value_ref, s32[1024,1]{1,0:T(8,128)S(1)} %copy.66.column_ref, ...), custom_call_target="tpu_custom_call" | custom-call | flops 1073741824 | bytes 2097152 | tf_op jit(solution)/shard_map/pallas_call | solution.py:92
  98.1 9.1 %collective-permute-done.9 = bf16[256,1024]{1,0:T(8,128)(2,1)} collective-permute-done((bf16[256,1024]{1,0:T(8,128)(2,1)}, bf16[256,1024]{1,0:T(8,128)(2,1)}, u32[]{:S(2)}, u32[]{:S(2)}) %collective-permute-start.9) | collective-permute-done | bytes 524320 | tf_op jit(solution)/shard_map/ppermute | solution.py:189
  107.1 10.4 %collective-permute-done.17 = bf16[256,1024]{1,0:T(8,128)(2,1)} collective-permute-done((bf16[256,1024]{1,0:T(8,128)(2,1)}, bf16[256,1024]{1,0:T(8,128)(2,1)}, u32[]{:S(2)}, u32[]{:S(2)}) %collective-permute-start.17) | collective-permute-done | bytes 524320 | tf_op jit(solution)/shard_map/ppermute | solution.py:189
  117.5 2.7 fusion.117
  123.3 11.9 %collective-permute-done.10 = bf16[256,1024]{1,0:T(8,128)(2,1)S(1)} collective-permute-done((bf16[256,1024]{1,0:T(8,128)(2,1)S(1)}, bf16[256,1024]{1,0:T(8,128)(2,1)S(1)}, u32[]{:S(2)}, u32[]{:S(2)}) %collective-permute-start.10) | collective-permute-done | bytes 524320 | tf_op jit(solution)/shard_map/ppermute | solution.py:189
  138.2 12.8 %collective-permute-done.18 = bf16[256,1024]{1,0:T(8,128)(2,1)} collective-permute-done((bf16[256,1024]{1,0:T(8,128)(2,1)}, bf16[256,1024]{1,0:T(8,128)(2,1)}, u32[]{:S(2)}, u32[]{:S(2)}) %collective-permute-start.18) | collective-permute-done | bytes 524320 | tf_op jit(solution)/shard_map/ppermute | solution.py:189
  153.4 7.5 %fusion.4 = (bf16[1024,1024]{1,0:T(8,128)(2,1)}, bf16[1024,1024]{1,0:T(8,128)(2,1)}) fusion(f32[1024]{0:T(1024)S(1)} %dynamic_slice.40, bf16[1024,1024]{1,0:T(8,128)(2,1)} %all-gather.3.cloned.1.call-done, bf16[512,1024]{1,0:T(8,128)(2,1)} %collective-permute-done.11, bf16[256,1024]{1,0:T(8,128)(2,1)} %copy-done.53, bf16[256,1024]{1,0:T(8,128)(2,1)} %copy-done.42), kind=kOutput, calls=%fused_computation.6 | convolution fusion | flops 2166358016 | bytes 8392704 | tf_op jit(solution)/shard_map/dot_general | solution.py:17
  160.9 13.4 %all-gather.5.cloned.1.call-done = bf16[1024,1024]{0,1:T(8,128)(2,1)} async-done(((bf16[128,1024]{0,1:T(8,128)(2,1)}), bf16[1024,1024]{0,1:T(8,128)(2,1)}) %all-gather.5.cloned.1.call-update) | async-done | bytes 2097168 | tf_op jit(solution)/shard_map/all_gather | solution.py:310
  174.3 3.2 convolution_convert_fusion.6
  181.6 4.4 fusion.9
  192.9 9.3 %collective-permute-done.13 = bf16[256,1024]{1,0:T(8,128)(2,1)S(1)} collective-permute-done((bf16[256,1024]{1,0:T(8,128)(2,1)S(1)}, bf16[256,1024]{1,0:T(8,128)(2,1)S(1)}, u32[]{:S(2)}, u32[]{:S(2)}) %collective-permute-start.13) | collective-permute-done | bytes 524320 | tf_op jit(solution)/shard_map/ppermute | solution.py:189
  202.2 10.8 %collective-permute-done.21 = bf16[256,1024]{1,0:T(8,128)(2,1)S(1)} collective-permute-done((bf16[256,1024]{1,0:T(8,128)(2,1)S(1)}, bf16[256,1024]{1,0:T(8,128)(2,1)S(1)}, u32[]{:S(2)}, u32[]{:S(2)}) %collective-permute-start.21) | collective-permute-done | bytes 524320 | tf_op jit(solution)/shard_map/ppermute | solution.py:189
  219.5 12.0 %collective-permute-done.22 = bf16[256,1024]{1,0:T(8,128)(2,1)S(1)} collective-permute-done((bf16[256,1024]{1,0:T(8,128)(2,1)S(1)}, bf16[256,1024]{1,0:T(8,128)(2,1)S(1)}, u32[]{:S(2)}, u32[]{:S(2)}) %collective-permute-start.22) | collective-permute-done | bytes 524320 | tf_op jit(solution)/shard_map/ppermute | solution.py:189
  233.3 12.9 %collective-permute-done.30 = bf16[256,1024]{1,0:T(8,128)(2,1)S(1)} collective-permute-done((bf16[256,1024]{1,0:T(8,128)(2,1)S(1)}, bf16[256,1024]{1,0:T(8,128)(2,1)S(1)}, u32[]{:S(2)}, u32[]{:S(2)}) %collective-permute-start.30) | collective-permute-done | bytes 524320 | tf_op jit(solution)/shard_map/ppermute | solution.py:189
  246.4 2.4 multiply_convert_fusion.1
  255.8 2.6 multiply_convert_fusion
  259.9 4.4 fusion.126
  264.3 4.9 %add_convert_fusion = bf16[1024,1024]{0,1:T(8,128)(2,1)S(1)} fusion(f32[1024,1024]{0,1:T(8,128)} %fusion.126, bf16[1024,1024]{1,0:T(8,128)(2,1)S(1)} %multiply_convert_fusion.1, bf16[512,1024]{1,0:T(8,128)(2,1)} %collective-permute-done.11, bf16[256,1024]{1,0:T(8,128)(2,1)S(1)} %copy-done.54, bf16[256,1024]{1,0:T(8,128)(2,1)S(1)} %copy-done.43), kind=kOutput, calls=%fused_computation.15 | convolution fusion | flops 2155872256 | bytes 10485760 | tf_op jit(solution)/shard_map/dot_general | solution.py:21
  272.0 13.0 %collective-permute-done.33 = bf16[256,1024]{1,0:T(8,128)(2,1)S(1)} collective-permute-done((bf16[256,1024]{1,0:T(8,128)(2,1)S(1)}, bf16[256,1024]{1,0:T(8,128)(2,1)S(1)}, u32[]{:S(2)}, u32[]{:S(2)}) %collective-permute-start.33) | collective-permute-done | bytes 524320 | tf_op jit(solution)/shard_map/ppermute | solution.py:189
  286.8 2.9 fusion.125
  289.7 10.0 %collective-permute-done.26 = bf16[256,1024]{1,0:T(8,128)(2,1)S(1)} collective-permute-done((bf16[256,1024]{1,0:T(8,128)(2,1)S(1)}, bf16[256,1024]{1,0:T(8,128)(2,1)S(1)}, u32[]{:S(2)}, u32[]{:S(2)}) %collective-permute-start.26) | collective-permute-done | bytes 524320 | tf_op jit(solution)/shard_map/ppermute | solution.py:189
  302.0 2.6 add_convert_fusion.1
  304.6 11.1 %collective-permute-done.34 = bf16[256,1024]{1,0:T(8,128)(2,1)S(1)} collective-permute-done((bf16[256,1024]{1,0:T(8,128)(2,1)S(1)}, bf16[256,1024]{1,0:T(8,128)(2,1)S(1)}, u32[]{:S(2)}, u32[]{:S(2)}) %collective-permute-start.34) | collective-permute-done | bytes 524320 | tf_op jit(solution)/shard_map/ppermute | solution.py:189
  319.6 18.0 %shard_map.307 = (bf16[1024,256]{1,0:T(8,128)(2,1)S(1)}, bf16[1024,256]{1,0:T(8,128)(2,1)S(1)}, bf16[1024,256]{1,0:T(8,128)(2,1)S(1)}) custom-call(bf16[1024,256]{1,0:T(8,128)(2,1)S(1)} %copy-done.5, bf16[1024,256]{1,0:T(8,128)(2,1)S(1)} %copy-done.3, bf16[1024,256]{1,0:T(8,128)(2,1)S(1)} %copy-done.1, ...), custom_call_target="tpu_custom_call" | custom-call | flops 2684354560 | bytes 3670016 | tf_op jit(solution)/shard_map/pallas_call | solution.py:158
  341.1 2.5 pad_maximum_fusion
  343.6 6.5 %copy.77 = bf16[1024,2048]{1,0:T(8,128)(2,1)} copy(bf16[1024,2048]{0,1:T(8,128)(2,1)} %pad_maximum_fusion) | data formatting | bytes 8388608
  354.3 2.4 convert_add_fusion.3
  359.7 18.4 %shard_map.308 = (bf16[1024,256]{1,0:T(8,128)(2,1)S(1)}, bf16[1024,256]{1,0:T(8,128)(2,1)S(1)}, bf16[1024,256]{1,0:T(8,128)(2,1)S(1)}) custom-call(bf16[1024,256]{1,0:T(8,128)(2,1)S(1)} %get-tuple-element.150.query_ref, bf16[1024,256]{1,0:T(8,128)(2,1)S(1)} %get-tuple-element.149.key_ref, bf16[1024,256]{1,0:T(8,128)(2,1)S(1)} %get-tuple-element.148.value_ref, ...), custom_call_target="tpu_custom_call" | custom-call | flops 2684354560 | bytes 3670016 | tf_op jit(solution)/shard_map/pallas_call | solution.py:158
  381.2 3.4 fusion.68
  384.6 3.0 add_convert_fusion.2
  389.2 3.3 reshape_reshape.11
  394.9 4.4 fusion.121
  399.4 4.6 copy.80
  403.9 4.6 copy.79
  411.5 4.1 collective-permute-done.43
  416.7 6.0 %collective-permute-done.44 = f32[96,128]{1,0:T(8,128)S(1)} collective-permute-done((f32[96,128]{1,0:T(8,128)S(1)}, f32[96,128]{1,0:T(8,128)S(1)}, u32[]{:S(2)}, u32[]{:S(2)}) %collective-permute-start.44) | collective-permute-done | bytes 49184 | tf_op jit(solution)/shard_map/ppermute | solution.py:189
  426.1 15.0 %collective-permute-done.45 = f32[96,128]{1,0:T(8,128)S(1)} collective-permute-done((f32[96,128]{1,0:T(8,128)S(1)}, f32[96,128]{1,0:T(8,128)S(1)}, u32[]{:S(2)}, u32[]{:S(2)}) %collective-permute-start.45) | collective-permute-done | bytes 49184 | tf_op jit(solution)/shard_map/ppermute | solution.py:189
  447.4 9.0 %collective-permute-done.39 = bf16[2,128,1024]{2,1,0:T(8,128)(2,1)S(1)} collective-permute-done((bf16[2,128,1024]{2,1,0:T(8,128)(2,1)S(1)}, bf16[2,128,1024]{2,1,0:T(8,128)(2,1)S(1)}, u32[]{:S(2)}, u32[]{:S(2)}) %collective-permute-start.39) | collective-permute-done | bytes 524320 | tf_op jit(solution)/shard_map/ppermute | solution.py:189
  460.9 9.2 %collective-permute-done.40 = bf16[1,128,1024]{2,1,0:T(8,128)(2,1)S(1)} collective-permute-done((bf16[1,128,1024]{2,1,0:T(8,128)(2,1)S(1)}, bf16[1,128,1024]{2,1,0:T(8,128)(2,1)S(1)}, u32[]{:S(2)}, u32[]{:S(2)}) %collective-permute-start.40) | collective-permute-done | bytes 262176 | tf_op jit(solution)/shard_map/ppermute | solution.py:189
  (379 shorter events, 117.4 us)
Async XLA Ops:
  7.2 146.1 %all-gather.3.cloned.1.call-start = ((), (), s32[]{:S(2)}) async-start(), calls=%async_computation.1 | async-start | bytes 2359296 | tf_op jit(solution)/shard_map/all_gather | solution.py:309
  8.3 8.6 %collective-permute-start.5 = (bf16[1,128,256]{2,1,0:T(8,128)(2,1)S(1)}, bf16[1,128,256]{2,1,0:T(8,128)(2,1)S(1)}, u32[]{:S(2)}, u32[]{:S(2)}) collective-permute-start(bf16[1,128,256]{2,1,0:T(8,128)(2,1)S(1)} %bitcast.262), channel_id=1, source_target_pairs={{0,16},{4,20},{8,24},{12,28},{16,0},{20,4},{24,8},{28,12},{1,17},{... | collective-permute-start | bytes 196616 | tf_op jit(solution)/shard_map/ppermute | solution.py:189
  13.3 11.6 %collective-permute-start.2 = (bf16[1,128,768]{2,1,0:T(8,128)(2,1)S(1)}, bf16[1,128,768]{2,1,0:T(8,128)(2,1)S(1)}, u32[]{:S(2)}, u32[]{:S(2)}) collective-permute-start(bf16[1,128,768]{2,1,0:T(8,128)(2,1)S(1)} %maximum_bitcast_fusion.1), channel_id=1, source_target_pairs={{0,16},{4,20},{8,24},{12,28},{16,0},{20,4},{24,8},{28,12},{1,17},{... | collective-permute-start | bytes 589832 | tf_op jit(solution)/shard_map/ppermute | solution.py:189
  14.7 24.6 %collective-permute-start = (bf16[256,1024]{1,0:T(8,128)(2,1)S(1)}, bf16[256,1024]{1,0:T(8,128)(2,1)}, u32[]{:S(2)}, u32[]{:S(2)}) collective-permute-start(bf16[256,1024]{1,0:T(8,128)(2,1)S(1)} %get-tuple-element.163), channel_id=1, source_target_pairs={{0,2},{1,3},{2,0},{3,1},{4,6},{5,7},{6,4},{7,5},{8,10},{9,11},{10,... | collective-permute-start | bytes 1572872 | tf_op jit(solution)/shard_map/ppermute | solution.py:189
  16.5 25.1 %collective-permute-start.14 = (bf16[256,1024]{1,0:T(8,128)(2,1)S(1)}, bf16[256,1024]{1,0:T(8,128)(2,1)}, u32[]{:S(2)}, u32[]{:S(2)}) collective-permute-start(bf16[256,1024]{1,0:T(8,128)(2,1)S(1)} %get-tuple-element.164), channel_id=1, source_target_pairs={{0,2},{1,3},{2,0},{3,1},{4,6},{5,7},{6,4},{7,5},{8,10},{9,11},{10,... | collective-permute-start | bytes 1572872 | tf_op jit(solution)/shard_map/ppermute | solution.py:189
  16.9 10.8 %collective-permute-start.6 = (bf16[2,128,256]{2,1,0:T(8,128)(2,1)S(1)}, bf16[2,128,256]{2,1,0:T(8,128)(2,1)S(1)}, u32[]{:S(2)}, u32[]{:S(2)}) collective-permute-start(bf16[2,128,256]{2,1,0:T(8,128)(2,1)S(1)} %maximum_bitcast_fusion.2), channel_id=1, source_target_pairs={{0,8},{4,12},{8,0},{12,4},{16,24},{20,28},{24,16},{28,20},{1,9},{5... | collective-permute-start | bytes 393224 | tf_op jit(solution)/shard_map/ppermute | solution.py:189
  25.1 10.8 %collective-permute-start.3 = (bf16[2,128,768]{2,1,0:T(8,128)(2,1)S(1)}, bf16[2,128,768]{2,1,0:T(8,128)(2,1)S(1)}, u32[]{:S(2)}, u32[]{:S(2)}) collective-permute-start(bf16[2,128,768]{2,1,0:T(8,128)(2,1)S(1)} %maximum_bitcast_fusion), channel_id=1, source_target_pairs={{0,8},{4,12},{8,0},{12,4},{16,24},{20,28},{24,16},{28,20},{1,9},{5... | collective-permute-start | bytes 1179656 | tf_op jit(solution)/shard_map/ppermute | solution.py:189
  27.8 12.7 %collective-permute-start.7 = (bf16[4,128,256]{2,1,0:T(8,128)(2,1)S(1)}, bf16[4,128,256]{2,1,0:T(8,128)(2,1)}, u32[]{:S(2)}, u32[]{:S(2)}) collective-permute-start(bf16[4,128,256]{2,1,0:T(8,128)(2,1)S(1)} %bitcast.260), channel_id=1, source_target_pairs={{0,4},{4,0},{8,12},{12,8},{16,20},{20,16},{24,28},{28,24},{1,5},{5... | collective-permute-start | bytes 786440 | tf_op jit(solution)/shard_map/ppermute | solution.py:189
  36.0 18.6 %collective-permute-start.4 = (bf16[4,128,768]{2,1,0:T(8,128)(2,1)S(1)}, bf16[4,128,768]{2,1,0:T(8,128)(2,1)}, u32[]{:S(2)}, u32[]{:S(2)}) collective-permute-start(bf16[4,128,768]{2,1,0:T(8,128)(2,1)S(1)} %bitcast.253), channel_id=1, source_target_pairs={{0,4},{4,0},{8,12},{12,8},{16,20},{20,16},{24,28},{28,24},{1,5},{5... | collective-permute-start | bytes 2359304 | tf_op jit(solution)/shard_map/ppermute | solution.py:189
  40.4 15.7 %collective-permute-start.1 = (bf16[512,1024]{1,0:T(8,128)(2,1)S(1)}, bf16[512,1024]{1,0:T(8,128)(2,1)S(1)}, u32[]{:S(2)}, u32[]{:S(2)}) collective-permute-start(bf16[512,1024]{1,0:T(8,128)(2,1)S(1)} %pad_maximum_fusion.12), channel_id=1, source_target_pairs={{0,1},{1,0},{2,3},{3,2},{4,5},{5,4},{6,7},{7,6},{8,9},{9,8},{10,11... | collective-permute-start | bytes 3145736 | tf_op jit(solution)/shard_map/ppermute | solution.py:189
  44.0 28.2 %collective-permute-start.15 = (bf16[512,1024]{1,0:T(8,128)(2,1)}, bf16[512,1024]{1,0:T(8,128)(2,1)}, u32[]{:S(2)}, u32[]{:S(2)}) collective-permute-start(bf16[512,1024]{1,0:T(8,128)(2,1)} %pad_maximum_fusion.14), channel_id=1, source_target_pairs={{0,1},{1,0},{2,3},{3,2},{4,5},{5,4},{6,7},{7,6},{8,9},{9,8},{10,11... | collective-permute-start | bytes 3145736 | tf_op jit(solution)/shard_map/ppermute | solution.py:189
  71.9 4.2 collective-permute-start.8
  71.9 102.4 %all-gather.5.cloned.1.call-start = ((), (), s32[]{:S(2)}) async-start(), calls=%async_computation.2 | async-start | bytes 2359296 | tf_op jit(solution)/shard_map/all_gather | solution.py:310
  91.5 2.8 collective-permute-start.16
  92.0 15.1 %collective-permute-start.9 = (bf16[256,1024]{1,0:T(8,128)(2,1)}, bf16[256,1024]{1,0:T(8,128)(2,1)}, u32[]{:S(2)}, u32[]{:S(2)}) collective-permute-start(bf16[256,1024]{1,0:T(8,128)(2,1)} %slice.522), channel_id=1, source_target_pairs={{0,2},{1,3},{2,0},{3,1},{4,6},{5,7},{6,4},{7,5},{8,10},{9,11},{10,... | collective-permute-start | bytes 1572872 | tf_op jit(solution)/shard_map/ppermute | solution.py:189
  96.3 21.2 %collective-permute-start.17 = (bf16[256,1024]{1,0:T(8,128)(2,1)}, bf16[256,1024]{1,0:T(8,128)(2,1)}, u32[]{:S(2)}, u32[]{:S(2)}) collective-permute-start(bf16[256,1024]{1,0:T(8,128)(2,1)} %slice.520), channel_id=1, source_target_pairs={{0,2},{1,3},{2,0},{3,1},{4,6},{5,7},{6,4},{7,5},{8,10},{9,11},{10,... | collective-permute-start | bytes 1572872 | tf_op jit(solution)/shard_map/ppermute | solution.py:189
  97.5 374.3 %reduce-scatter.4.cloned.1.call-start = ((), (), s32[]{:S(2)}) async-start(), calls=%async_computation.3 | async-start | bytes 4718592
  122.1 13.1 %collective-permute-start.10 = (bf16[256,1024]{1,0:T(8,128)(2,1)S(1)}, bf16[256,1024]{1,0:T(8,128)(2,1)S(1)}, u32[]{:S(2)}, u32[]{:S(2)}) collective-permute-start(bf16[256,1024]{1,0:T(8,128)(2,1)S(1)} %get-tuple-element.189), channel_id=1, source_target_pairs={{0,2},{1,3},{2,0},{3,1},{4,6},{5,7},{6,4},{7,5},{8,10},{9,11},{10,... | collective-permute-start | bytes 1572872 | tf_op jit(solution)/shard_map/ppermute | solution.py:189
  136.4 17.0 %collective-permute-start.11 = (bf16[512,1024]{1,0:T(8,128)(2,1)}, bf16[512,1024]{1,0:T(8,128)(2,1)}, u32[]{:S(2)}, u32[]{:S(2)}) collective-permute-start(bf16[512,1024]{1,0:T(8,128)(2,1)} %pad_maximum_fusion.13), channel_id=1, source_target_pairs={{0,1},{1,0},{2,3},{3,2},{4,5},{5,4},{6,7},{7,6},{8,9},{9,8},{10,11... | collective-permute-start | bytes 3145736 | tf_op jit(solution)/shard_map/ppermute | solution.py:189
  136.4 14.7 %collective-permute-start.18 = (bf16[256,1024]{1,0:T(8,128)(2,1)}, bf16[256,1024]{1,0:T(8,128)(2,1)}, u32[]{:S(2)}, u32[]{:S(2)}) collective-permute-start(bf16[256,1024]{1,0:T(8,128)(2,1)} %get-tuple-element.190), channel_id=1, source_target_pairs={{0,2},{1,3},{2,0},{3,1},{4,6},{5,7},{6,4},{7,5},{8,10},{9,11},{10,... | collective-permute-start | bytes 1572872 | tf_op jit(solution)/shard_map/ppermute | solution.py:189
  153.4 24.2 %collective-permute-start.19 = (bf16[512,1024]{1,0:T(8,128)(2,1)}, bf16[512,1024]{1,0:T(8,128)(2,1)}, u32[]{:S(2)}, u32[]{:S(2)}) collective-permute-start(bf16[512,1024]{1,0:T(8,128)(2,1)} %pad_maximum_fusion.15), channel_id=1, source_target_pairs={{0,1},{1,0},{2,3},{3,2},{4,5},{5,4},{6,7},{7,6},{8,9},{9,8},{10,11... | collective-permute-start | bytes 3145736 | tf_op jit(solution)/shard_map/ppermute | solution.py:189
  177.5 2.7 collective-permute-start.12
  187.3 2.7 collective-permute-start.20
  187.4 14.8 %collective-permute-start.13 = (bf16[256,1024]{1,0:T(8,128)(2,1)S(1)}, bf16[256,1024]{1,0:T(8,128)(2,1)S(1)}, u32[]{:S(2)}, u32[]{:S(2)}) collective-permute-start(bf16[256,1024]{1,0:T(8,128)(2,1)S(1)} %slice.521), channel_id=1, source_target_pairs={{0,2},{1,3},{2,0},{3,1},{4,6},{5,7},{6,4},{7,5},{8,10},{9,11},{10,... | collective-permute-start | bytes 1572872 | tf_op jit(solution)/shard_map/ppermute | solution.py:189
  191.4 21.6 %collective-permute-start.21 = (bf16[256,1024]{1,0:T(8,128)(2,1)S(1)}, bf16[256,1024]{1,0:T(8,128)(2,1)S(1)}, u32[]{:S(2)}, u32[]{:S(2)}) collective-permute-start(bf16[256,1024]{1,0:T(8,128)(2,1)S(1)} %slice.519), channel_id=1, source_target_pairs={{0,2},{1,3},{2,0},{3,1},{4,6},{5,7},{6,4},{7,5},{8,10},{9,11},{10,... | collective-permute-start | bytes 1572872 | tf_op jit(solution)/shard_map/ppermute | solution.py:189
  218.0 13.6 %collective-permute-start.22 = (bf16[256,1024]{1,0:T(8,128)(2,1)S(1)}, bf16[256,1024]{1,0:T(8,128)(2,1)S(1)}, u32[]{:S(2)}, u32[]{:S(2)}) collective-permute-start(bf16[256,1024]{1,0:T(8,128)(2,1)S(1)} %convert_element_type.246), channel_id=1, source_target_pairs={{0,2},{1,3},{2,0},{3,1},{4,6},{5,7},{6,4},{7,5},{8,10},{9,11},{10,... | collective-permute-start | bytes 1572872 | tf_op jit(solution)/shard_map/ppermute | solution.py:189
  231.7 14.7 %collective-permute-start.23 = (bf16[512,1024]{1,0:T(8,128)(2,1)S(1)}, bf16[512,1024]{1,0:T(8,128)(2,1)S(1)}, u32[]{:S(2)}, u32[]{:S(2)}) collective-permute-start(bf16[512,1024]{1,0:T(8,128)(2,1)S(1)} %pad_maximum_fusion.17), channel_id=1, source_target_pairs={{0,1},{1,0},{2,3},{3,2},{4,5},{5,4},{6,7},{7,6},{8,9},{9,8},{10,11... | collective-permute-start | bytes 3145736 | tf_op jit(solution)/shard_map/ppermute | solution.py:189
  231.8 14.4 %collective-permute-start.30 = (bf16[256,1024]{1,0:T(8,128)(2,1)S(1)}, bf16[256,1024]{1,0:T(8,128)(2,1)S(1)}, u32[]{:S(2)}, u32[]{:S(2)}) collective-permute-start(bf16[256,1024]{1,0:T(8,128)(2,1)S(1)} %convert_element_type.259), channel_id=1, source_target_pairs={{0,2},{1,3},{2,0},{3,1},{4,6},{5,7},{6,4},{7,5},{8,10},{9,11},{10,... | collective-permute-start | bytes 1572872 | tf_op jit(solution)/shard_map/ppermute | solution.py:189
  246.3 4.5 collective-permute-start.31
  250.1 2.8 collective-permute-start.24
  254.3 17.0 %collective-permute-start.25 = (bf16[256,1024]{1,0:T(8,128)(2,1)S(1)}, bf16[256,1024]{1,0:T(8,128)(2,1)S(1)}, u32[]{:S(2)}, u32[]{:S(2)}) collective-permute-start(bf16[256,1024]{1,0:T(8,128)(2,1)S(1)} %slice.518), channel_id=1, source_target_pairs={{0,2},{1,3},{2,0},{3,1},{4,6},{5,7},{6,4},{7,5},{8,10},{9,11},{10,... | collective-permute-start | bytes 1572872 | tf_op jit(solution)/shard_map/ppermute | solution.py:189
  259.7 9.5 %collective-permute-start.32 = (bf16[512,1024]{1,0:T(8,128)(2,1)S(1)}, bf16[512,1024]{1,0:T(8,128)(2,1)S(1)}, u32[]{:S(2)}, u32[]{:S(2)}) collective-permute-start(bf16[512,1024]{1,0:T(8,128)(2,1)S(1)} %convolution_convert_fusion.2), channel_id=1, source_target_pairs={{0,1},{1,0},{2,3},{3,2},{4,5},{5,4},{6,7},{7,6},{8,9},{9,8},{10,11... | collective-permute-start | bytes 3145736 | tf_op jit(solution)/shard_map/ppermute | solution.py:189
  270.7 14.3 %collective-permute-start.33 = (bf16[256,1024]{1,0:T(8,128)(2,1)S(1)}, bf16[256,1024]{1,0:T(8,128)(2,1)S(1)}, u32[]{:S(2)}, u32[]{:S(2)}) collective-permute-start(bf16[256,1024]{1,0:T(8,128)(2,1)S(1)} %slice.516), channel_id=1, source_target_pairs={{0,2},{1,3},{2,0},{3,1},{4,6},{5,7},{6,4},{7,5},{8,10},{9,11},{10,... | collective-permute-start | bytes 1572872 | tf_op jit(solution)/shard_map/ppermute | solution.py:189
  286.2 13.6 %collective-permute-start.26 = (bf16[256,1024]{1,0:T(8,128)(2,1)S(1)}, bf16[256,1024]{1,0:T(8,128)(2,1)S(1)}, u32[]{:S(2)}, u32[]{:S(2)}) collective-permute-start(bf16[256,1024]{1,0:T(8,128)(2,1)S(1)} %convert_element_type.252), channel_id=1, source_target_pairs={{0,2},{1,3},{2,0},{3,1},{4,6},{5,7},{6,4},{7,5},{8,10},{9,11},{10,... | collective-permute-start | bytes 1572872 | tf_op jit(solution)/shard_map/ppermute | solution.py:189
  299.8 17.8 %collective-permute-start.27 = (bf16[512,1024]{1,0:T(8,128)(2,1)S(1)}, bf16[512,1024]{1,0:T(8,128)(2,1)S(1)}, u32[]{:S(2)}, u32[]{:S(2)}) collective-permute-start(bf16[512,1024]{1,0:T(8,128)(2,1)S(1)} %pad_maximum_fusion.18), channel_id=1, source_target_pairs={{0,1},{1,0},{2,3},{3,2},{4,5},{5,4},{6,7},{7,6},{8,9},{9,8},{10,11... | collective-permute-start | bytes 3145736 | tf_op jit(solution)/shard_map/ppermute | solution.py:189
  301.3 14.4 %collective-permute-start.34 = (bf16[256,1024]{1,0:T(8,128)(2,1)S(1)}, bf16[256,1024]{1,0:T(8,128)(2,1)S(1)}, u32[]{:S(2)}, u32[]{:S(2)}) collective-permute-start(bf16[256,1024]{1,0:T(8,128)(2,1)S(1)} %convert_element_type.265), channel_id=1, source_target_pairs={{0,2},{1,3},{2,0},{3,1},{4,6},{5,7},{6,4},{7,5},{8,10},{9,11},{10,... | collective-permute-start | bytes 1572872 | tf_op jit(solution)/shard_map/ppermute | solution.py:189
  317.6 34.6 %collective-permute-start.35 = (bf16[512,1024]{1,0:T(8,128)(2,1)}, bf16[512,1024]{1,0:T(8,128)(2,1)}, u32[]{:S(2)}, u32[]{:S(2)}) collective-permute-start(bf16[512,1024]{1,0:T(8,128)(2,1)} %pad_maximum_fusion.20), channel_id=1, source_target_pairs={{0,1},{1,0},{2,3},{3,2},{4,5},{5,4},{6,7},{7,6},{8,9},{9,8},{10,11... | collective-permute-start | bytes 3145736 | tf_op jit(solution)/shard_map/ppermute | solution.py:189
  341.1 13.1 %collective-permute-start.28 = (bf16[512,1024]{1,0:T(8,128)(2,1)}, bf16[512,1024]{1,0:T(8,128)(2,1)}, u32[]{:S(2)}, u32[]{:S(2)}) collective-permute-start(bf16[512,1024]{1,0:T(8,128)(2,1)} %convolution_convert_fusion.1), channel_id=1, source_target_pairs={{0,1},{1,0},{2,3},{3,2},{4,5},{5,4},{6,7},{7,6},{8,9},{9,8},{10,11... | collective-permute-start | bytes 3145736 | tf_op jit(solution)/shard_map/ppermute | solution.py:189
  394.4 14.1 %collective-permute-start.41 = (f32[96,128]{1,0:T(8,128)S(1)}, f32[96,128]{1,0:T(8,128)S(1)}, u32[]{:S(2)}, u32[]{:S(2)}) collective-permute-start(f32[96,128]{1,0:T(8,128)S(1)} %bitcast.263), channel_id=1, source_target_pairs={{0,2},{1,3},{2,0},{3,1},{4,6},{5,7},{6,4},{7,5},{8,10},{9,11},{10,... | collective-permute-start | bytes 147464 | tf_op jit(solution)/shard_map/ppermute | solution.py:189
  409.0 33.4 %collective-permute-start.38 = (bf16[4,128,1024]{2,1,0:T(8,128)(2,1)S(1)}, bf16[4,128,1024]{2,1,0:T(8,128)(2,1)S(1)}, u32[]{:S(2)}, u32[]{:S(2)}) collective-permute-start(bf16[4,128,1024]{2,1,0:T(8,128)(2,1)S(1)} %select_bitcast_fusion), channel_id=1, source_target_pairs={{0,4},{4,0},{8,12},{12,8},{16,20},{20,16},{24,28},{28,24},{1,5},{5... | collective-permute-start | bytes 3145736 | tf_op jit(solution)/shard_map/ppermute | solution.py:189
  410.5 5.1 %collective-permute-start.43 = (f32[96,128]{1,0:T(8,128)S(1)}, f32[96,128]{1,0:T(8,128)S(1)}, u32[]{:S(2)}, u32[]{:S(2)}) collective-permute-start(f32[96,128]{1,0:T(8,128)S(1)} %fusion.165), channel_id=1, source_target_pairs={{0,16},{4,20},{8,24},{12,28},{16,0},{20,4},{24,8},{28,12},{1,17},{... | collective-permute-start | bytes 147464 | tf_op jit(solution)/shard_map/ppermute | solution.py:189
  415.5 7.2 %collective-permute-start.44 = (f32[96,128]{1,0:T(8,128)S(1)}, f32[96,128]{1,0:T(8,128)S(1)}, u32[]{:S(2)}, u32[]{:S(2)}) collective-permute-start(f32[96,128]{1,0:T(8,128)S(1)} %add.366), channel_id=1, source_target_pairs={{0,8},{4,12},{8,0},{12,4},{16,24},{20,28},{24,16},{28,20},{1,9},{5... | collective-permute-start | bytes 147464 | tf_op jit(solution)/shard_map/ppermute | solution.py:189
  422.7 18.4 %collective-permute-start.45 = (f32[96,128]{1,0:T(8,128)S(1)}, f32[96,128]{1,0:T(8,128)S(1)}, u32[]{:S(2)}, u32[]{:S(2)}) collective-permute-start(f32[96,128]{1,0:T(8,128)S(1)} %add.367), channel_id=1, source_target_pairs={{0,4},{4,0},{8,12},{12,8},{16,20},{20,16},{24,28},{28,24},{1,5},{5... | collective-permute-start | bytes 147464 | tf_op jit(solution)/shard_map/ppermute | solution.py:189
  424.6 18.5 %collective-permute-start.29 = (bf16[256,1024]{1,0:T(8,128)(2,1)S(1)}, bf16[256,1024]{1,0:T(8,128)(2,1)S(1)}, u32[]{:S(2)}, u32[]{:S(2)}) collective-permute-start(bf16[256,1024]{1,0:T(8,128)(2,1)S(1)} %copy-done.52), channel_id=1, source_target_pairs={{0,2},{1,3},{2,0},{3,1},{4,6},{5,7},{6,4},{7,5},{8,10},{9,11},{10,... | collective-permute-start | bytes 1572872 | tf_op jit(solution)/shard_map/ppermute | solution.py:189
  426.1 18.5 %collective-permute-start.36 = (bf16[512,1024]{1,0:T(8,128)(2,1)S(1)}, bf16[512,1024]{1,0:T(8,128)(2,1)S(1)}, u32[]{:S(2)}, u32[]{:S(2)}) collective-permute-start(bf16[512,1024]{1,0:T(8,128)(2,1)S(1)} %convolution_convert_fusion), channel_id=1, source_target_pairs={{0,1},{1,0},{2,3},{3,2},{4,5},{5,4},{6,7},{7,6},{8,9},{9,8},{10,11... | collective-permute-start | bytes 3145736 | tf_op jit(solution)/shard_map/ppermute | solution.py:189
  443.0 13.4 %collective-permute-start.39 = (bf16[2,128,1024]{2,1,0:T(8,128)(2,1)S(1)}, bf16[2,128,1024]{2,1,0:T(8,128)(2,1)S(1)}, u32[]{:S(2)}, u32[]{:S(2)}) collective-permute-start(bf16[2,128,1024]{2,1,0:T(8,128)(2,1)S(1)} %fusion.82), channel_id=1, source_target_pairs={{0,8},{4,12},{8,0},{12,4},{16,24},{20,28},{24,16},{28,20},{1,9},{5... | collective-permute-start | bytes 1572872 | tf_op jit(solution)/shard_map/ppermute | solution.py:189
  445.7 13.4 %collective-permute-start.37 = (bf16[256,1024]{1,0:T(8,128)(2,1)S(1)}, bf16[256,1024]{1,0:T(8,128)(2,1)S(1)}, u32[]{:S(2)}, u32[]{:S(2)}) collective-permute-start(bf16[256,1024]{1,0:T(8,128)(2,1)S(1)} %slice.515), channel_id=1, source_target_pairs={{0,2},{1,3},{2,0},{3,1},{4,6},{5,7},{6,4},{7,5},{8,10},{9,11},{10,... | collective-permute-start | bytes 1572872 | tf_op jit(solution)/shard_map/ppermute | solution.py:189
  456.8 13.4 %collective-permute-start.40 = (bf16[1,128,1024]{2,1,0:T(8,128)(2,1)S(1)}, bf16[1,128,1024]{2,1,0:T(8,128)(2,1)S(1)}, u32[]{:S(2)}, u32[]{:S(2)}) collective-permute-start(bf16[1,128,1024]{2,1,0:T(8,128)(2,1)S(1)} %fusion.84), channel_id=1, source_target_pairs={{0,16},{4,20},{8,24},{12,28},{16,0},{20,4},{24,8},{28,12},{1,17},{... | collective-permute-start | bytes 786440 | tf_op jit(solution)/shard_map/ppermute | solution.py:189
  (76 other events, 586.1 us)
Sparse Core Ops, SparseCore 0:
  72.0 50.5 all-gather.2
  124.7 49.5 all-gather.4
  350.2 90.1 reduce-scatter.3
